TPU v7x, 512 devices: a whole 4x8x8 slice. The times are simulated.
512 devices in a mesh: row: 16 (over z, core), col: 32 (over y, x).
Axes of the slice: x: 4, y: 8, z: 8, core: 2. Of those that a mesh axis runs over, the one named last changes fastest.
Arguments:
- row_bases: float32 [16, 512, 4096], P('row', 'col'), may hold values from -4 to 4, as said below
- col_bases: float32 [32, 256, 4096], P('col', 'row'), may hold values from -4 to 4, as said below
- row_transfer: float32 [16, 1024, 4096], P('row', 'col'), may hold values from -1 to 1, as said below
- col_transfer: float32 [32, 512, 4096], P('col', 'row'), may hold values from -1 to 1, as said below
- row_order: int32 [16, 32, 16], P('row', 'col'), may hold values from 0 to 15, each once within a row
- col_order: int32 [32, 16, 16], P('col', 'row'), may hold values from 0 to 15, each once within a row
- leaf_pattern: int32 [16, 64, 64], P('row', 'col'), may hold values from 0 to 15
- leaf_blocks: bfloat16 [16, 2048, 4096], P('row', 'col'), may hold values from -6 to 6
- root_rows: int32 [16, 32, 32], P('row', 'col'), may hold values from 0 to 31
- root_cols: int32 [16, 32, 32], P('row', 'col'), may hold values from 0 to 15
- root_blocks: bfloat16 [16, 1024, 4096], P('row', 'col'), may hold values from -6 to 6
Outputs:
- leaf_coupled: float32 [16, 2048, 4096], P('row', 'col')
- root_coupled: float32 [16, 1024, 4096], P('row', 'col')
- row_upper_r: float32 [16, 32, 4096], P('row', 'col')
- col_upper_r: float32 [32, 16, 4096], P('col', 'row')
Inputs may be any that keep to these rules, and one draw needn't show every extreme that they name: `row_bases`: every leaf basis has full column rank and every Gram matrix of both trees is well conditioned. `col_bases`: every leaf basis has full column rank and every Gram matrix of both trees is well conditioned. `row_transfer`: every transfer matrix is invertible. `col_transfer`: every transfer matrix is invertible.
All inputs are finite; a program needn't handle non-finite values.
Results may differ from a plain program's by a relative error of at most 0.0003.
Values sent between devices are 32-bit elements; how exact they have to be, the bound alone decides.
A program may use at most 64 MiB of HBM per device.

v0:
```python
import jax
import jax.numpy as jnp
from jax import lax
from jax.sharding import PartitionSpec as P

LEAF = 64
RANK = 64
LEAF_DEV = 16


def from_partner(value, axis, bit):
    return lax.ppermute(value, axis, [(i, i ^ 1 << bit) for i in range(lax.axis_size(axis))])


def matmul_high(first_matrix, second_matrix):
    return jnp.matmul(first_matrix, second_matrix, precision=lax.Precision.HIGHEST)


def flipped(matrix):
    return jnp.swapaxes(matrix, -1, -2)


def sandwich(gram, transfer):
    return matmul_high(flipped(transfer), matmul_high(gram, transfer))


def upper_factor(gram):
    return flipped(jnp.linalg.cholesky(gram))


def as_row(matrix):
    return matrix.reshape(1, RANK * RANK)


def as_square(vector):
    return vector.reshape(-1, RANK, RANK)


def local_tree(bases, transfer, order):
    leaf_basis = bases.reshape(LEAF_DEV, LEAF, RANK)
    leaf_gram = jnp.einsum("pla,plc->pac", leaf_basis, leaf_basis, precision=lax.Precision.HIGHEST)
    matrices = transfer.reshape(2 * LEAF_DEV, RANK, RANK)
    leaf_picks = order.reshape(LEAF_DEV)
    node_gram = leaf_gram[leaf_picks]
    node_up = matrices[leaf_picks]
    node_count = LEAF_DEV
    offset = LEAF_DEV
    while node_count > 1:
        contribution = sandwich(node_gram, node_up)
        node_gram = contribution[0::2] + contribution[1::2]
        node_count = node_count // 2
        node_up = matrices[offset : offset + node_count]
        offset = offset + node_count
    return (upper_factor(leaf_gram), node_gram[0], node_up[0], matrices[2 * LEAF_DEV - 1])


def doubling(
    dev_gram,
    dev_up,
    inner_up,
    inner_size,
    outer_size,
    inner_place,
    outer_place,
    inner_move,
    outer_move,
):
    current_gram = dev_gram
    current_up = dev_up
    first_inner = inner_up
    highest = dev_gram
    inner_depth = inner_size.bit_length() - 1
    outer_depth = outer_size.bit_length() - 1
    place = outer_place * inner_size + inner_place
    for height in range(inner_depth + outer_depth):
        contribution = sandwich(current_gram, current_up)
        if height < inner_depth:
            received, received_first = inner_move(as_row(contribution), as_row(first_inner), height)
        else:
            received, received_first = outer_move(
                as_row(contribution), as_row(first_inner), height - inner_depth
            )
        span = 1 << height
        upper_half = place // span % 2 == 1
        current_gram = contribution + received.reshape(RANK, RANK)
        highest = jnp.where(place % (2 * span) == span, current_gram, highest)
        partner_first = received_first.reshape(RANK, RANK)
        current_up = jnp.where(upper_half, first_inner, partner_first)
        first_inner = jnp.where(upper_half, partner_first, first_inner)
    return jnp.where(place == 0, current_gram, highest)


def couple(left_table, right_table, left_picks, right_picks, blocks):
    squares = blocks.reshape(-1, RANK, RANK).astype(jnp.float32)
    projected = matmul_high(
        matmul_high(left_table[left_picks], squares), flipped(right_table[right_picks])
    )
    return projected.reshape(1, -1, RANK * RANK)


def body(
    row_bases,
    col_bases,
    row_transfer,
    col_transfer,
    row_order,
    col_order,
    leaf_pattern,
    leaf_blocks,
    root_rows,
    root_cols,
    root_blocks,
):
    row_leaf_r, row_gram, row_up, row_inner = local_tree(row_bases, row_transfer, row_order)
    col_leaf_r, col_gram, col_up, col_inner = local_tree(col_bases, col_transfer, col_order)
    leaf_coupled = couple(
        row_leaf_r, col_leaf_r, leaf_pattern[0, 0], leaf_pattern[0, 1], leaf_blocks
    )
    place_row = lax.axis_index("row")
    place_col = lax.axis_index("col")
    row_high = doubling(
        row_gram,
        row_up,
        row_inner,
        lax.axis_size("col"),
        lax.axis_size("row"),
        place_col,
        place_row,
        lambda first_part, second_part, level: from_partner(
            (first_part, second_part), "col", level
        ),
        lambda first_part, second_part, level: from_partner(
            (first_part, second_part), "row", level
        ),
    )
    col_high = doubling(
        col_gram,
        col_up,
        col_inner,
        lax.axis_size("row"),
        lax.axis_size("col"),
        place_row,
        place_col,
        lambda first_part, second_part, level: from_partner(
            (first_part, second_part), "row", level
        ),
        lambda first_part, second_part, level: from_partner(
            (first_part, second_part), "col", level
        ),
    )
    row_root_r = as_square(
        lax.all_gather(as_row(upper_factor(row_gram)), "col", axis=0, tiled=True)
    )
    col_root_r = as_square(
        lax.all_gather(as_row(upper_factor(col_gram)), "row", axis=0, tiled=True)
    )
    root_coupled = couple(row_root_r, col_root_r, root_rows[0, 0], root_cols[0, 0], root_blocks)
    row_upper_r = upper_factor(row_high).reshape(1, 1, RANK * RANK)
    col_upper_r = upper_factor(col_high).reshape(1, 1, RANK * RANK)
    return (leaf_coupled, root_coupled, row_upper_r, col_upper_r)


def solution(mesh):
    return jax.shard_map(
        body,
        mesh=mesh,
        in_specs=(
            P("row", "col", None),
            P("col", "row", None),
            P("row", "col", None),
            P("col", "row", None),
            P("row", "col", None),
            P("col", "row", None),
            P("row", "col", None),
            P("row", "col", None),
            P("row", "col", None),
            P("row", "col", None),
            P("row", "col", None),
        ),
        out_specs=(
            P("row", "col", None),
            P("row", "col", None),
            P("row", "col", None),
            P("col", "row", None),
        ),
        check_vma=False,
    )
```

profile of v0, /device:TPU:8, one launch (start us, length us, event | category | flops | bytes accessed | tf_op | source)
XLA Modules:
  0.0 512.6 jit_solution(7395350178116248555)
XLA Ops:
  17.3 3.4 collective-permute-start
  34.8 5.8 %cholesky.150 = f32[64,64]{1,0:T(8,128)S(1)} custom-call(f32[64,64]{1,0:T(8,128)S(1)} %fusion.26), custom_call_target="Cholesky" | custom-call | tf_op jit(solution)/shard_map/jit(cholesky)/cholesky | solution.py:28
  42.1 23.9 %all-gather.1 = f32[16,1,4096]{2,1,0:T(1,128)S(1)} all-gather(f32[1,1,4096]{2,1,0:T(1,128)S(1)} %reshape.611), channel_id=1, replica_groups=mesh['row'=16,'col'=32] {'row'}, dimensions={0}, use_global_device_ids=true | all-gather | bytes 278528 | tf_op jit(solution)/shard_map/all_gather | solution.py:155
  66.9 5.8 %cholesky.139 = f32[64,64]{1,0:T(8,128)S(1)} custom-call(f32[64,64]{1,0:T(8,128)S(1)} %fusion.27), custom_call_target="Cholesky" | custom-call | tf_op jit(solution)/shard_map/jit(cholesky)/cholesky | solution.py:28
  74.3 49.6 %all-gather = f32[32,1,4096]{2,1,0:T(1,128)S(1)} all-gather(f32[1,1,4096]{2,1,0:T(1,128)S(1)} %reshape.609), channel_id=1, replica_groups=mesh['row'=16,'col'=32] {'col'}, dimensions={0}, use_global_device_ids=true | all-gather | bytes 540672 | tf_op jit(solution)/shard_map/all_gather | solution.py:152
  131.7 95.2 %custom-call.6 = f32[16,64,64]{2,1,0:T(8,128)} custom-call(f32[16,64,64]{2,1,0:T(8,128)} %fusion.1), custom_call_target="Cholesky" | custom-call | tf_op jit(solution)/shard_map/jit(cholesky)/cholesky | solution.py:28
  226.9 94.5 %custom-call.7 = f32[16,64,64]{2,1,0:T(8,128)} custom-call(f32[16,64,64]{2,1,0:T(8,128)S(1)} %fusion), custom_call_target="Cholesky" | custom-call | tf_op jit(solution)/shard_map/jit(cholesky)/cholesky | solution.py:28
  332.4 4.4 fusion.101
  338.7 4.5 fusion.103
  356.3 3.9 collective-permute-start.26
  360.2 4.2 collective-permute-start.1
  364.4 3.2 collective-permute-start.9
  372.3 3.3 collective-permute-start.2
  377.4 4.3 collective-permute-start.20
  382.6 4.1 collective-permute-start.3
  391.2 5.7 %collective-permute-start.4 = (f32[1,4096]{1,0:T(1,128)S(1)}, f32[1,4096]{1,0:T(1,128)S(1)}, u32[]{:S(2)}, u32[]{:S(2)}) collective-permute-start(f32[1,4096]{1,0:T(1,128)S(1)} %get-tuple-element.49), channel_id=1, source_target_pairs={{0,16},{1,17},{2,18},{3,19},{4,20},{5,21},{6,22},{7,23},{8,24},{9,... | collective-permute-start | bytes 49160 | tf_op jit(solution)/shard_map/ppermute | solution.py:12
  397.8 4.0 collective-permute-start.22
  405.7 3.0 collective-permute-start.23
  412.4 3.1 collective-permute-start.24
  416.5 4.8 collective-permute-start.7
  430.9 4.9 collective-permute-start.28
  437.4 3.5 collective-permute-start.11
  442.3 3.7 collective-permute-start.29
  447.6 4.5 collective-permute-start.12
  453.5 4.0 collective-permute-start.30
  466.9 3.9 collective-permute-start.14
  472.2 3.1 collective-permute-start.32
  476.9 4.4 collective-permute-start.15
  482.7 4.7 collective-permute-start.33
  489.0 5.3 %collective-permute-start.16 = (f32[1,4096]{1,0:T(1,128)S(1)}, f32[1,4096]{1,0:T(1,128)S(1)}, u32[]{:S(2)}, u32[]{:S(2)}) collective-permute-start(f32[1,4096]{1,0:T(1,128)S(1)} %reshape.515), channel_id=1, source_target_pairs={{0,256},{32,288},{64,320},{96,352},{128,384},{160,416},{192,448},{... | collective-permute-start | bytes 49160 | tf_op jit(solution)/shard_map/ppermute | solution.py:12
  495.4 5.8 %cholesky.172 = f32[64,64]{1,0:T(8,128)S(1)} custom-call(f32[64,64]{1,0:T(8,128)S(1)} %fusion.28), custom_call_target="Cholesky" | custom-call | tf_op jit(solution)/shard_map/jit(cholesky)/cholesky | solution.py:28
  504.4 5.8 %cholesky.161 = f32[64,64]{1,0:T(8,128)S(1)} custom-call(f32[64,64]{1,0:T(8,128)S(1)} %fusion.29), custom_call_target="Cholesky" | custom-call | tf_op jit(solution)/shard_map/jit(cholesky)/cholesky | solution.py:28
  (363 shorter events, 124.8 us)
Async XLA Ops:
  2.5 344.3 %collective-permute-start.17 = (f32[1,4096]{1,0:T(1,128)}, f32[1,4096]{1,0:T(1,128)}, u32[]{:S(2)}, u32[]{:S(2)}) collective-permute-start(f32[1,4096]{1,0:T(1,128)} %get-tuple-element.26), channel_id=1, source_target_pairs={{0,32},{32,0},{64,96},{96,64},{128,160},{160,128},{192,224},{224,1... | collective-permute-start | bytes 49160 | tf_op jit(solution)/shard_map/ppermute | solution.py:12
  14.9 336.1 %collective-permute-start.25 = (f32[1,4096]{1,0:T(1,128)}, f32[1,4096]{1,0:T(1,128)}, u32[]{:S(2)}, u32[]{:S(2)}) collective-permute-start(f32[1,4096]{1,0:T(1,128)} %reshape.526), channel_id=1, source_target_pairs={{0,32},{32,0},{64,96},{96,64},{128,160},{160,128},{192,224},{224,1... | collective-permute-start | bytes 49160 | tf_op jit(solution)/shard_map/ppermute | solution.py:12
  17.3 335.6 %collective-permute-start = (f32[1,4096]{1,0:T(1,128)}, f32[1,4096]{1,0:T(1,128)}, u32[]{:S(2)}, u32[]{:S(2)}) collective-permute-start(f32[1,4096]{1,0:T(1,128)} %get-tuple-element.70), channel_id=1, source_target_pairs={{0,1},{1,0},{2,3},{3,2},{4,5},{5,4},{6,7},{7,6},{8,9},{9,8},{10,11... | collective-permute-start | bytes 49160 | tf_op jit(solution)/shard_map/ppermute | solution.py:12
  30.3 324.4 %collective-permute-start.8 = (f32[1,4096]{1,0:T(1,128)S(1)}, f32[1,4096]{1,0:T(1,128)S(1)}, u32[]{:S(2)}, u32[]{:S(2)}) collective-permute-start(f32[1,4096]{1,0:T(1,128)S(1)} %reshape.499), channel_id=1, source_target_pairs={{0,1},{1,0},{2,3},{3,2},{4,5},{5,4},{6,7},{7,6},{8,9},{9,8},{10,11... | collective-permute-start | bytes 49160 | tf_op jit(solution)/shard_map/ppermute | solution.py:12
  348.9 18.7 %collective-permute-start.18 = (f32[1,4096]{1,0:T(1,128)S(1)}, f32[1,4096]{1,0:T(1,128)S(1)}, u32[]{:S(2)}, u32[]{:S(2)}) collective-permute-start(f32[1,4096]{1,0:T(1,128)S(1)} %get-tuple-element.29), channel_id=1, source_target_pairs={{0,64},{32,96},{64,0},{96,32},{128,192},{160,224},{192,128},{224,1... | collective-permute-start | bytes 49160 | tf_op jit(solution)/shard_map/ppermute | solution.py:12
  356.3 15.1 %collective-permute-start.26 = (f32[1,4096]{1,0:T(1,128)S(1)}, f32[1,4096]{1,0:T(1,128)S(1)}, u32[]{:S(2)}, u32[]{:S(2)}) collective-permute-start(f32[1,4096]{1,0:T(1,128)S(1)} %reshape.528), channel_id=1, source_target_pairs={{0,64},{32,96},{64,0},{96,32},{128,192},{160,224},{192,128},{224,1... | collective-permute-start | bytes 49160 | tf_op jit(solution)/shard_map/ppermute | solution.py:12
  360.2 10.3 %collective-permute-start.1 = (f32[1,4096]{1,0:T(1,128)S(1)}, f32[1,4096]{1,0:T(1,128)S(1)}, u32[]{:S(2)}, u32[]{:S(2)}) collective-permute-start(f32[1,4096]{1,0:T(1,128)S(1)} %get-tuple-element.43), channel_id=1, source_target_pairs={{0,2},{1,3},{2,0},{3,1},{4,6},{5,7},{6,4},{7,5},{8,10},{9,11},{10,... | collective-permute-start | bytes 49160 | tf_op jit(solution)/shard_map/ppermute | solution.py:12
  364.4 11.3 %collective-permute-start.9 = (f32[1,4096]{1,0:T(1,128)S(1)}, f32[1,4096]{1,0:T(1,128)S(1)}, u32[]{:S(2)}, u32[]{:S(2)}) collective-permute-start(f32[1,4096]{1,0:T(1,128)S(1)} %reshape.501), channel_id=1, source_target_pairs={{0,2},{1,3},{2,0},{3,1},{4,6},{5,7},{6,4},{7,5},{8,10},{9,11},{10,... | collective-permute-start | bytes 49160 | tf_op jit(solution)/shard_map/ppermute | solution.py:12
  368.4 8.3 %collective-permute-start.19 = (f32[1,4096]{1,0:T(1,128)S(1)}, f32[1,4096]{1,0:T(1,128)S(1)}, u32[]{:S(2)}, u32[]{:S(2)}) collective-permute-start(f32[1,4096]{1,0:T(1,128)S(1)} %get-tuple-element.31), channel_id=1, source_target_pairs={{0,128},{32,160},{64,192},{96,224},{128,0},{160,32},{192,64},{224,... | collective-permute-start | bytes 49160 | tf_op jit(solution)/shard_map/ppermute | solution.py:12
  372.3 9.3 %collective-permute-start.2 = (f32[1,4096]{1,0:T(1,128)S(1)}, f32[1,4096]{1,0:T(1,128)S(1)}, u32[]{:S(2)}, u32[]{:S(2)}) collective-permute-start(f32[1,4096]{1,0:T(1,128)S(1)} %get-tuple-element.45), channel_id=1, source_target_pairs={{0,4},{1,5},{2,6},{3,7},{4,0},{5,1},{6,2},{7,3},{8,12},{9,13},{10,... | collective-permute-start | bytes 49160 | tf_op jit(solution)/shard_map/ppermute | solution.py:12
  377.4 9.5 %collective-permute-start.20 = (f32[1,4096]{1,0:T(1,128)S(1)}, f32[1,4096]{1,0:T(1,128)S(1)}, u32[]{:S(2)}, u32[]{:S(2)}) collective-permute-start(f32[1,4096]{1,0:T(1,128)S(1)} %get-tuple-element.33), channel_id=1, source_target_pairs={{0,256},{32,288},{64,320},{96,352},{128,384},{160,416},{192,448},{... | collective-permute-start | bytes 49160 | tf_op jit(solution)/shard_map/ppermute | solution.py:12
  382.6 7.8 %collective-permute-start.3 = (f32[1,4096]{1,0:T(1,128)S(1)}, f32[1,4096]{1,0:T(1,128)S(1)}, u32[]{:S(2)}, u32[]{:S(2)}) collective-permute-start(f32[1,4096]{1,0:T(1,128)S(1)} %get-tuple-element.47), channel_id=1, source_target_pairs={{0,8},{1,9},{2,10},{3,11},{4,12},{5,13},{6,14},{7,15},{8,0},{9,1},... | collective-permute-start | bytes 49160 | tf_op jit(solution)/shard_map/ppermute | solution.py:12
  387.7 9.4 %collective-permute-start.21 = (f32[1,4096]{1,0:T(1,128)S(1)}, f32[1,4096]{1,0:T(1,128)S(1)}, u32[]{:S(2)}, u32[]{:S(2)}) collective-permute-start(f32[1,4096]{1,0:T(1,128)S(1)} %get-tuple-element.35), channel_id=1, source_target_pairs={{0,1},{1,0},{2,3},{3,2},{4,5},{5,4},{6,7},{7,6},{8,9},{9,8},{10,11... | collective-permute-start | bytes 49160 | tf_op jit(solution)/shard_map/ppermute | solution.py:12
  391.2 10.6 %collective-permute-start.4 = (f32[1,4096]{1,0:T(1,128)S(1)}, f32[1,4096]{1,0:T(1,128)S(1)}, u32[]{:S(2)}, u32[]{:S(2)}) collective-permute-start(f32[1,4096]{1,0:T(1,128)S(1)} %get-tuple-element.49), channel_id=1, source_target_pairs={{0,16},{1,17},{2,18},{3,19},{4,20},{5,21},{6,22},{7,23},{8,24},{9,... | collective-permute-start | bytes 49160 | tf_op jit(solution)/shard_map/ppermute | solution.py:12
  397.8 7.1 %collective-permute-start.22 = (f32[1,4096]{1,0:T(1,128)S(1)}, f32[1,4096]{1,0:T(1,128)S(1)}, u32[]{:S(2)}, u32[]{:S(2)}) collective-permute-start(f32[1,4096]{1,0:T(1,128)S(1)} %get-tuple-element.37), channel_id=1, source_target_pairs={{0,2},{1,3},{2,0},{3,1},{4,6},{5,7},{6,4},{7,5},{8,10},{9,11},{10,... | collective-permute-start | bytes 49160 | tf_op jit(solution)/shard_map/ppermute | solution.py:12
  409.6 6.0 %collective-permute-start.6 = (f32[1,4096]{1,0:T(1,128)S(1)}, f32[1,4096]{1,0:T(1,128)S(1)}, u32[]{:S(2)}, u32[]{:S(2)}) collective-permute-start(f32[1,4096]{1,0:T(1,128)S(1)} %get-tuple-element.53), channel_id=1, source_target_pairs={{0,64},{32,96},{64,0},{96,32},{128,192},{160,224},{192,128},{224,1... | collective-permute-start | bytes 49160 | tf_op jit(solution)/shard_map/ppermute | solution.py:12
  412.4 9.0 %collective-permute-start.24 = (f32[1,4096]{1,0:T(1,128)S(1)}, f32[1,4096]{1,0:T(1,128)S(1)}, u32[]{:S(2)}, u32[]{:S(2)}) collective-permute-start(f32[1,4096]{1,0:T(1,128)S(1)} %get-tuple-element.41), channel_id=1, source_target_pairs={{0,8},{1,9},{2,10},{3,11},{4,12},{5,13},{6,14},{7,15},{8,0},{9,1},... | collective-permute-start | bytes 49160 | tf_op jit(solution)/shard_map/ppermute | solution.py:12
  416.5 8.6 %collective-permute-start.7 = (f32[1,4096]{1,0:T(1,128)S(1)}, f32[1,4096]{1,0:T(1,128)S(1)}, u32[]{:S(2)}, u32[]{:S(2)}) collective-permute-start(f32[1,4096]{1,0:T(1,128)S(1)} %get-tuple-element.55), channel_id=1, source_target_pairs={{0,128},{32,160},{64,192},{96,224},{128,0},{160,32},{192,64},{224,... | collective-permute-start | bytes 49160 | tf_op jit(solution)/shard_map/ppermute | solution.py:12
  422.9 6.6 %collective-permute-start.27 = (f32[1,4096]{1,0:T(1,128)S(1)}, f32[1,4096]{1,0:T(1,128)S(1)}, u32[]{:S(2)}, u32[]{:S(2)}) collective-permute-start(f32[1,4096]{1,0:T(1,128)S(1)} %reshape.530), channel_id=1, source_target_pairs={{0,128},{32,160},{64,192},{96,224},{128,0},{160,32},{192,64},{224,... | collective-permute-start | bytes 49160 | tf_op jit(solution)/shard_map/ppermute | solution.py:12
  426.6 9.2 %collective-permute-start.10 = (f32[1,4096]{1,0:T(1,128)S(1)}, f32[1,4096]{1,0:T(1,128)S(1)}, u32[]{:S(2)}, u32[]{:S(2)}) collective-permute-start(f32[1,4096]{1,0:T(1,128)S(1)} %reshape.503), channel_id=1, source_target_pairs={{0,4},{1,5},{2,6},{3,7},{4,0},{5,1},{6,2},{7,3},{8,12},{9,13},{10,... | collective-permute-start | bytes 49160 | tf_op jit(solution)/shard_map/ppermute | solution.py:12
  430.9 10.0 %collective-permute-start.28 = (f32[1,4096]{1,0:T(1,128)S(1)}, f32[1,4096]{1,0:T(1,128)S(1)}, u32[]{:S(2)}, u32[]{:S(2)}) collective-permute-start(f32[1,4096]{1,0:T(1,128)S(1)} %reshape.532), channel_id=1, source_target_pairs={{0,256},{32,288},{64,320},{96,352},{128,384},{160,416},{192,448},{... | collective-permute-start | bytes 49160 | tf_op jit(solution)/shard_map/ppermute | solution.py:12
  437.4 8.6 %collective-permute-start.11 = (f32[1,4096]{1,0:T(1,128)S(1)}, f32[1,4096]{1,0:T(1,128)S(1)}, u32[]{:S(2)}, u32[]{:S(2)}) collective-permute-start(f32[1,4096]{1,0:T(1,128)S(1)} %reshape.505), channel_id=1, source_target_pairs={{0,8},{1,9},{2,10},{3,11},{4,12},{5,13},{6,14},{7,15},{8,0},{9,1},... | collective-permute-start | bytes 49160 | tf_op jit(solution)/shard_map/ppermute | solution.py:12
  442.3 9.8 %collective-permute-start.29 = (f32[1,4096]{1,0:T(1,128)S(1)}, f32[1,4096]{1,0:T(1,128)S(1)}, u32[]{:S(2)}, u32[]{:S(2)}) collective-permute-start(f32[1,4096]{1,0:T(1,128)S(1)} %reshape.534), channel_id=1, source_target_pairs={{0,1},{1,0},{2,3},{3,2},{4,5},{5,4},{6,7},{7,6},{8,9},{9,8},{10,11... | collective-permute-start | bytes 49160 | tf_op jit(solution)/shard_map/ppermute | solution.py:12
  447.6 9.9 %collective-permute-start.12 = (f32[1,4096]{1,0:T(1,128)S(1)}, f32[1,4096]{1,0:T(1,128)S(1)}, u32[]{:S(2)}, u32[]{:S(2)}) collective-permute-start(f32[1,4096]{1,0:T(1,128)S(1)} %reshape.507), channel_id=1, source_target_pairs={{0,16},{1,17},{2,18},{3,19},{4,20},{5,21},{6,22},{7,23},{8,24},{9,... | collective-permute-start | bytes 49160 | tf_op jit(solution)/shard_map/ppermute | solution.py:12
  453.5 7.5 %collective-permute-start.30 = (f32[1,4096]{1,0:T(1,128)S(1)}, f32[1,4096]{1,0:T(1,128)S(1)}, u32[]{:S(2)}, u32[]{:S(2)}) collective-permute-start(f32[1,4096]{1,0:T(1,128)S(1)} %reshape.536), channel_id=1, source_target_pairs={{0,2},{1,3},{2,0},{3,1},{4,6},{5,7},{6,4},{7,5},{8,10},{9,11},{10,... | collective-permute-start | bytes 49160 | tf_op jit(solution)/shard_map/ppermute | solution.py:12
  459.1 6.3 %collective-permute-start.13 = (f32[1,4096]{1,0:T(1,128)S(1)}, f32[1,4096]{1,0:T(1,128)S(1)}, u32[]{:S(2)}, u32[]{:S(2)}) collective-permute-start(f32[1,4096]{1,0:T(1,128)S(1)} %reshape.509), channel_id=1, source_target_pairs={{0,32},{32,0},{64,96},{96,64},{128,160},{160,128},{192,224},{224,1... | collective-permute-start | bytes 49160 | tf_op jit(solution)/shard_map/ppermute | solution.py:12
  462.4 8.5 %collective-permute-start.31 = (f32[1,4096]{1,0:T(1,128)S(1)}, f32[1,4096]{1,0:T(1,128)S(1)}, u32[]{:S(2)}, u32[]{:S(2)}) collective-permute-start(f32[1,4096]{1,0:T(1,128)S(1)} %reshape.538), channel_id=1, source_target_pairs={{0,4},{1,5},{2,6},{3,7},{4,0},{5,1},{6,2},{7,3},{8,12},{9,13},{10,... | collective-permute-start | bytes 49160 | tf_op jit(solution)/shard_map/ppermute | solution.py:12
  466.9 8.4 %collective-permute-start.14 = (f32[1,4096]{1,0:T(1,128)S(1)}, f32[1,4096]{1,0:T(1,128)S(1)}, u32[]{:S(2)}, u32[]{:S(2)}) collective-permute-start(f32[1,4096]{1,0:T(1,128)S(1)} %reshape.511), channel_id=1, source_target_pairs={{0,64},{32,96},{64,0},{96,32},{128,192},{160,224},{192,128},{224,1... | collective-permute-start | bytes 49160 | tf_op jit(solution)/shard_map/ppermute | solution.py:12
  472.2 9.1 %collective-permute-start.32 = (f32[1,4096]{1,0:T(1,128)S(1)}, f32[1,4096]{1,0:T(1,128)S(1)}, u32[]{:S(2)}, u32[]{:S(2)}) collective-permute-start(f32[1,4096]{1,0:T(1,128)S(1)} %reshape.540), channel_id=1, source_target_pairs={{0,8},{1,9},{2,10},{3,11},{4,12},{5,13},{6,14},{7,15},{8,0},{9,1},... | collective-permute-start | bytes 49160 | tf_op jit(solution)/shard_map/ppermute | solution.py:12
  476.9 10.6 %collective-permute-start.15 = (f32[1,4096]{1,0:T(1,128)S(1)}, f32[1,4096]{1,0:T(1,128)S(1)}, u32[]{:S(2)}, u32[]{:S(2)}) collective-permute-start(f32[1,4096]{1,0:T(1,128)S(1)} %reshape.513), channel_id=1, source_target_pairs={{0,128},{32,160},{64,192},{96,224},{128,0},{160,32},{192,64},{224,... | collective-permute-start | bytes 49160 | tf_op jit(solution)/shard_map/ppermute | solution.py:12
  482.7 11.6 %collective-permute-start.33 = (f32[1,4096]{1,0:T(1,128)S(1)}, f32[1,4096]{1,0:T(1,128)S(1)}, u32[]{:S(2)}, u32[]{:S(2)}) collective-permute-start(f32[1,4096]{1,0:T(1,128)S(1)} %reshape.542), channel_id=1, source_target_pairs={{0,16},{1,17},{2,18},{3,19},{4,20},{5,21},{6,22},{7,23},{8,24},{9,... | collective-permute-start | bytes 49160 | tf_op jit(solution)/shard_map/ppermute | solution.py:12
  489.0 14.3 %collective-permute-start.16 = (f32[1,4096]{1,0:T(1,128)S(1)}, f32[1,4096]{1,0:T(1,128)S(1)}, u32[]{:S(2)}, u32[]{:S(2)}) collective-permute-start(f32[1,4096]{1,0:T(1,128)S(1)} %reshape.515), channel_id=1, source_target_pairs={{0,256},{32,288},{64,320},{96,352},{128,384},{160,416},{192,448},{... | collective-permute-start | bytes 49160 | tf_op jit(solution)/shard_map/ppermute | solution.py:12
  (18 other events, 365.3 us)
where the time goes:
time: 523 us; the launch traced here: 513 us
  other arithmetic  251 us (48%)
  starting transfers between devices  117 us (22%)
  blocking collectives  73.4 us (14%)
  local copies, waits for them, and re-layouts  36.9 us (7%)
  matrix products  30.4 us (6%)
    another operation x17, other arithmetic, upper_factor(): return flipped(jnp.linalg.cholesky(gram))  216 us
    ppermute x34, starting transfers between devices, from_partner(): lax.ppermute(value, axis, [(i, i ^ 1 << bit) for i in range(lax.axis_size...  117 us
    all_gather x1, blocking collectives, body(): lax.all_gather(as_row(upper_factor(row_gram)), 'col', axis=0, tiled=True)  49.6 us
    dot_general x56, matrix products, matmul_high(): jnp.matmul(first_matrix, second_matrix, precision=lax.Precision.HIGHEST)  28.4 us
    ppermute x34, other arithmetic, from_partner(): lax.ppermute(value, axis, [(i, i ^ 1 << bit) for i in range(lax.axis_size...  27.1 us
    all_gather x1, blocking collectives, body(): lax.all_gather(as_row(upper_factor(col_gram)), 'row', axis=0, tiled=True)  23.9 us
  transfers between devices with their start and end apart: 34, of which 2 were waited for; matrix products, arithmetic and copies ran while one was open for 60% of the time, Pallas kernels for 0%

commit v1 on v0

v1 whole, which is shorter than its diff:
```python
import functools

import jax
import jax.numpy as jnp
from jax import lax
from jax.experimental import pallas as pl
from jax.experimental.pallas import tpu as pltpu
from jax.sharding import PartitionSpec as P

RANK = 64
LEAF_DEV = 16
LEAF_PAIRS = 64
ROOT_PAIRS = 32
N_ROW = 16
N_COL = 32
N_X = 4
N_Y = 8
GROUP = 24
BATCH = 2 * GROUP
MESH = pl.DeviceIdType.MESH
F32 = jnp.float32
BF16 = jnp.bfloat16


def split(value):
    high = value.astype(BF16)
    return high, (value - high.astype(F32)).astype(BF16)


def contract(left, right, left_dim, right_dim):
    return lax.dot_general(
        left, right, (((left_dim,), (right_dim,)), ((), ())), preferred_element_type=F32
    )


def product_tn(left, right):
    left_high, left_low = split(left)
    right_high, right_low = split(right)
    return contract(
        jnp.concatenate([left_high, left_high, left_low], 0),
        jnp.concatenate([right_high, right_low, right_high], 0),
        0,
        0,
    )


def product_nn(left, right):
    left_high, left_low = split(left)
    right_high, right_low = split(right)
    both = contract(jnp.concatenate([left_high, left_low], 0), right_high, 1, 0)
    rows = left.shape[0]
    return both[:rows] + both[rows:] + contract(left_high, right_low, 1, 0)


def sandwich(gram, transfer):
    return product_tn(transfer, product_nn(gram, transfer))


def pack(square):
    return jnp.concatenate([square[:32, :], square[32:, :]], 1)


def unpack(packed):
    return jnp.concatenate([packed[:, :RANK], packed[:, RANK:]], 0)


def level_of(place, depth):
    level = jnp.int32(depth)
    for k in range(depth - 1, 0, -1):
        level = jnp.where(lax.rem(place, 1 << k) == 1 << (k - 1), jnp.int32(k), level)
    return level


def span_of(place, depth):
    span = jnp.int32(1 << depth)
    for k in range(depth - 1, 0, -1):
        span = jnp.where(lax.rem(place, 1 << k) == 1 << (k - 1), jnp.int32(1 << k), span)
    return span


def fixed_level(place, depth):
    return depth if place == 0 else (place & -place).bit_length()


class Stage:
    def __init__(self, depth, place, taking_part, peer, refs):
        self.depth, self.size, self.place = depth, 1 << depth, place
        self.taking_part, self.peer = taking_part, peer
        (self.inner, self.terms, self.slots, self.inner_sent, self.inner_got, self.sent, self.got) = refs
        self.level = level_of(place, depth)
        self.span = span_of(place, depth)

    def inner_copy(self, target, level):
        return pltpu.make_async_remote_copy(
            self.own_inner,
            self.inner.at[level - 1],
            self.inner_sent.at[target],
            self.inner_got.at[level - 1],
            device_id=self.peer(target),
            device_id_type=MESH,
        )

    def each_inner_target(self, act):
        for target in range(self.size):
            same = lax.div(self.place, self.span) == lax.div(jnp.int32(target), self.span)
            wanted = (self.place != 0) & (self.place != target) & same
            if target != 0:
                wanted = wanted & (self.span < self.size)
            pl.when(self.taking_part & wanted)(functools.partial(act, target))

    def send_inner(self, own_inner):
        self.own_inner = own_inner
        self.each_inner_target(lambda target: self.inner_copy(target, self.level).start())

    def receive_inner(self):
        for level in range(1, self.depth + 1):
            half = 1 << (level - 1)
            if level < self.depth:
                mine = lax.rem(self.place, 2 * half) == half
                away = jnp.logical_not(mine)

                @pl.when(self.taking_part & mine)
                def _(level=level):
                    self.inner[level - 1] = self.own_inner[...]
            else:
                away = self.place == 0

            @pl.when(self.taking_part & away)
            def _(level=level):
                self.inner_copy(0, level).wait_recv()

    def make_terms(self, gram, transfer):
        path = transfer
        for level in range(1, self.depth + 1):
            self.terms[level - 1] = pack(sandwich(gram, path))
            if level < self.depth:
                path = product_nn(path, unpack(self.inner[level - 1]))

    def term_copy(self, target, sender):
        return pltpu.make_async_remote_copy(
            self.terms.at[fixed_level(target, self.depth) - 1],
            self.slots.at[sender],
            self.sent.at[target],
            self.got.at[sender],
            device_id=self.peer(target),
            device_id_type=MESH,
        )

    def each_target(self, act):
        for target in range(self.size):
            span = 1 << fixed_level(target, self.depth)
            wanted = (self.place != target) & (lax.div(self.place, span) == target // span)
            pl.when(self.taking_part & wanted)(functools.partial(act, target))

    def send_terms(self):
        self.each_target(lambda target: self.term_copy(target, self.place).start())

    def receive_terms(self, total_ref):
        @pl.when(self.taking_part)
        def _():
            total_ref[...] = self.terms[self.level - 1]

        for sender in range(self.size):
            same = lax.div(self.place, self.span) == lax.div(jnp.int32(sender), self.span)

            @pl.when(self.taking_part & (self.place != sender) & same)
            def _(sender=sender):
                self.term_copy(0, sender).wait_recv()
                total_ref[...] += self.slots[sender]

    def finish(self):
        self.each_inner_target(lambda target: self.inner_copy(target, self.level).wait_send())
        self.each_target(lambda target: self.term_copy(target, self.place).wait_send())


def to_lanes(gram_ref, batch_ref, count):
    flat = gram_ref.reshape(BATCH * RANK, 128)

    def step(j, carry):
        rows = flat[pl.ds(j, count, stride=RANK), :]
        batch_ref[j, :, :count] = rows.T[:RANK, :]
        return carry

    lax.fori_loop(0, RANK, step, 0, unroll=8)


def factor(batch_ref):
    for block in range(8):
        first = 8 * block
        columns = [batch_ref[first + c, first:, :] for c in range(8)]
        for c in range(8):
            pivot = columns[c][c : c + 1, :]
            column = columns[c] * lax.rsqrt(pivot)
            columns[c] = column
            batch_ref[first + c, first:, :] = column
            for later in range(c + 1, 8):
                columns[later] = columns[later] - column * column[later : later + 1, :]
        for other in range(block + 1, 8):

            def update(step, carry, first=first, other=other):
                j = 8 * other + step
                total = batch_ref[j, 8 * other :, :]
                for c in range(8):
                    total = total - batch_ref[first + c, 8 * other :, :] * batch_ref[first + c, pl.ds(j, 1), :]
                batch_ref[j, 8 * other :, :] = total
                return carry

            lax.fori_loop(0, 8, update, 0, unroll=4)


def from_lanes(batch_ref, factor_ref, counts):
    lane = lax.broadcasted_iota(jnp.int32, (1, 128), 1)
    column = jnp.where(lane < 32, 2 * lane, jnp.where(lane < 64, 2 * lane - 63, lane - 64))

    def step(j, carry):
        plane = batch_ref.at[j]
        values = jnp.concatenate(
            [plane[pl.ds(0, 32, stride=2), :], plane[pl.ds(1, 32, stride=2), :], plane[...]], 0
        ).T
        values = jnp.where(column >= j, values[: sum(counts)], 0.0)
        moved = lax.div(j, 2) + 32 * lax.rem(j, 2)
        factor_ref[pl.ds(moved, counts[0], stride=RANK), :] = values[: counts[0]]
        if len(counts) > 1:
            factor_ref[pl.ds(counts[0] * RANK + j, counts[1], stride=RANK), :] = values[counts[0] :]
        return carry

    lax.fori_loop(0, RANK, step, 0, unroll=4)


def couple(count, blocks_ref, stage_ref, left_ref, right_ref, left_pick, right_pick, out_ref):
    def step(group, carry):
        base = pl.multiple_of(group * 256, 256)
        stage_ref[...] = blocks_ref[pl.ds(base, 256), :].astype(F32)
        for pair in range(8):
            packed = stage_ref[pl.ds(pair, 32, stride=8), :].astype(BF16)
            square = unpack(packed)
            left = left_ref[left_pick(group * 8 + pair)]
            right = right_ref[right_pick(group * 8 + pair)]
            both = contract(left, square, 1, 0)
            high, low = split(both[:RANK] + both[RANK:])
            out = contract(jnp.concatenate([high, low], 0), right[:RANK], 1, 1)
            out = out[:RANK] + out[RANK:] + contract(high, right[RANK:], 1, 1)
            out_ref[pl.ds(base + pair, 32, stride=8), :] = pack(out)
        return carry

    lax.fori_loop(0, count // 8, step, 0)


def table_entry(value):
    return jnp.concatenate(split(value), 0)


STAGES = ((2, 3, 4), (4, 2, 3))


def kernel(
    row_order,
    col_order,
    leaf_pattern,
    root_rows,
    root_cols,
    row_bases_hbm,
    col_bases_hbm,
    row_transfer_hbm,
    col_transfer_hbm,
    leaf_blocks_hbm,
    root_blocks_hbm,
    leaf_out,
    root_out,
    row_out,
    col_out,
    bases,
    transfers,
    leaf_blocks,
    root_blocks,
    loads,
    natural,
    grams,
    nodes,
    batch,
    factors,
    leaf_left,
    leaf_right,
    root_left,
    root_right,
    block_stage,
    inner_own,
    highest,
    row_own,
    col_own,
    row_table,
    col_table,
    row_sent,
    row_got,
    col_sent,
    col_got,
    *stage_refs,
):
    place_row = lax.axis_index("row")
    place_col = lax.axis_index("col")
    copies = [
        pltpu.make_async_copy(source, target, loads.at[n])
        for n, (source, target) in enumerate(
            [
                (row_bases_hbm, bases.at[0]),
                (col_bases_hbm, bases.at[1]),
                (row_transfer_hbm, transfers.at[0]),
                (col_transfer_hbm, transfers.at[1]),
                (leaf_blocks_hbm, leaf_blocks),
                (root_blocks_hbm, root_blocks),
            ]
        )
    ]
    for copy in copies:
        copy.start()
    barrier = pltpu.get_barrier_semaphore()

    def greet(axis, size, place):
        def step(k, carry):
            pl.semaphore_signal(
                barrier, inc=1, device_id={axis: lax.rem(place + k, size)}, device_id_type=MESH
            )
            return carry

        lax.fori_loop(1, size, step, 0)

    greet("col", N_COL, place_col)
    greet("row", N_ROW, place_row)

    x_place = lax.rem(place_col, N_X)
    y_place = lax.div(place_col, N_X)
    always = place_row >= 0
    x_peer = lambda p: {"col": y_place * N_X + p}
    y_peer = lambda p: {"col": p * N_X}
    z_peer = lambda p: {"row": jnp.int32(p)}
    layout = (
        (
            (x_place, always, x_peer),
            (y_place, x_place == 0, y_peer),
            (place_row, place_col == 0, z_peer),
        ),
        (
            (place_row, always, z_peer),
            (x_place, place_row == 0, x_peer),
            (y_place, (place_row == 0) & (x_place == 0), y_peer),
        ),
    )
    stages = []
    for tree in range(2):
        stages.append([])
        for n in range(3):
            at = 7 * (3 * tree + n)
            stages[tree].append(Stage(STAGES[tree][n], *layout[tree][n], stage_refs[at : at + 7]))

    copies[2].wait()
    copies[3].wait()
    for tree in range(2):

        def lay_out(m, carry, tree=tree):
            rows = transfers[tree, pl.ds(lax.div(m, 8) * 256 + lax.rem(m, 8), 32, stride=8), :]
            place = natural.at[tree * 32 + m]
            place[pl.ds(0, 32, stride=2), :] = rows
            place[pl.ds(1, 32, stride=2), :] = pltpu.roll(rows, RANK, 1)
            return carry

        lax.fori_loop(0, 32, lay_out, 0, unroll=4)

    def transfer_of(tree, m):
        return natural[tree * 32 + m][:, :RANK]

    for tree in range(2):
        inner_own[tree] = pack(transfer_of(tree, 31))
    pl.semaphore_wait(barrier, N_COL + N_ROW - 2)
    for tree in range(2):
        for n in range(3):
            stages[tree][n].send_inner(inner_own.at[tree])

    copies[0].wait()
    copies[1].wait()

    def leaf_gram(leaf, carry):
        for tree in range(2):
            rows = bases[tree, pl.ds(lax.div(leaf, 8) * 256 + lax.rem(leaf, 8), 32, stride=8), :]
            basis = unpack(rows)
            grams[tree * GROUP + leaf, :, :RANK] = product_tn(basis, basis)
        return carry

    lax.fori_loop(0, LEAF_DEV, leaf_gram, 0, unroll=4)

    orders = (row_order, col_order)

    def first_level(q, carry):
        for tree in range(2):
            total = None
            for child in range(2):
                leaf = orders[tree][2 * q + child]
                term = sandwich(grams[tree * GROUP + leaf][:, :RANK], transfer_of(tree, leaf))
                total = term if total is None else total + term
            nodes[tree * 16 + q, :, :RANK] = total
        return carry

    lax.fori_loop(0, 8, first_level, 0, unroll=2)
    source, target, offset, count = 0, 8, 16, 8
    while count > 1:
        for tree in range(2):
            for q in range(count // 2):
                total = None
                for child in range(2):
                    node = 2 * q + child
                    term = sandwich(
                        nodes[tree * 16 + source + node][:, :RANK], transfer_of(tree, offset + node)
                    )
                    total = term if total is None else total + term
                if count > 2:
                    nodes[tree * 16 + target + q, :, :RANK] = total
                else:
                    grams[tree * GROUP + LEAF_DEV, :, :RANK] = total
        offset += count
        source, target, count = target, target + count // 2, count // 2

    for tree in range(2):
        stage = stages[tree][0]
        stage.receive_inner()
        stage.make_terms(grams[tree * GROUP + LEAF_DEV][:, :RANK], transfer_of(tree, 30))
        stage.send_terms()

    to_lanes(grams, batch, BATCH)
    factor(batch)
    from_lanes(batch, factors, (GROUP, GROUP))
    row_own[...] = pack(factors[LEAF_DEV * RANK : (LEAF_DEV + 1) * RANK, :RANK])
    col_own[...] = pack(factors[(GROUP + LEAF_DEV) * RANK : (GROUP + LEAF_DEV + 1) * RANK, RANK:])
    row_table[place_col] = row_own[...]
    col_table[place_row] = col_own[...]

    def table_copy(axis, size, place, own, table, sent, got, k, slot):
        return pltpu.make_async_remote_copy(
            own,
            table.at[slot],
            sent.at[k],
            got.at[slot],
            device_id={axis: lax.rem(place + k, size)},
            device_id_type=MESH,
        )

    row_parts = ("col", N_COL, place_col, row_own, row_table, row_sent, row_got)
    col_parts = ("row", N_ROW, place_row, col_own, col_table, col_sent, col_got)
    for parts in (row_parts, col_parts):

        def send(k, carry, parts=parts):
            table_copy(*parts, k, parts[2]).start()
            return carry

        lax.fori_loop(1, parts[1], send, 0)

    for leaf in range(LEAF_DEV):
        leaf_left[leaf] = table_entry(factors[leaf * RANK : (leaf + 1) * RANK, :RANK])
        leaf_right[leaf] = table_entry(factors[(GROUP + leaf) * RANK : (GROUP + leaf + 1) * RANK, RANK:])

    def climb(n):
        for tree in range(2):
            stages[tree][n - 1].receive_terms(highest.at[tree])
            stage = stages[tree][n]
            stage.receive_inner()

            @pl.when(stage.taking_part)
            def _(stage=stage, tree=tree, n=n):
                exit_transfer = unpack(stages[tree][n - 1].inner[stages[tree][n - 1].depth - 1])
                stage.make_terms(unpack(highest[tree]), exit_transfer)

            stage.send_terms()

    climb(1)
    copies[4].wait()
    couple(
        LEAF_PAIRS,
        leaf_blocks,
        block_stage,
        leaf_left,
        leaf_right,
        lambda pair: leaf_pattern[pair],
        lambda pair: leaf_pattern[LEAF_PAIRS + pair],
        leaf_out,
    )
    climb(2)

    for parts in (row_parts, col_parts):

        def receive(k, carry, parts=parts):
            size, place = parts[1], parts[2]
            table_copy(*parts, k, lax.rem(place + size - k, size)).wait_recv()
            return carry

        lax.fori_loop(1, parts[1], receive, 0)

    def convert(table, entries, count):
        def step(n, carry):
            entries[n] = table_entry(unpack(table[n]))
            return carry

        lax.fori_loop(0, count, step, 0, unroll=4)

    convert(row_table, root_left, N_COL)
    convert(col_table, root_right, N_ROW)
    copies[5].wait()
    couple(
        ROOT_PAIRS,
        root_blocks,
        block_stage,
        root_left,
        root_right,
        lambda pair: root_rows[pair],
        lambda pair: root_cols[pair],
        root_out,
    )

    for tree in range(2):
        stages[tree][2].receive_terms(highest.at[tree])
        grams[tree, :, :RANK] = unpack(highest[tree])
    to_lanes(grams, batch, 8)
    factor(batch)
    from_lanes(batch, factors, (8,))
    for tree, out in enumerate((row_out, col_out)):
        out[...] = pack(factors[tree * RANK : (tree + 1) * RANK, RANK:])

    for tree in range(2):
        for n in range(3):
            stages[tree][n].finish()
    for parts in (row_parts, col_parts):

        def drain(k, carry, parts=parts):
            table_copy(*parts, k, parts[2]).wait_send()
            return carry

        lax.fori_loop(1, parts[1], drain, 0)


def tiled(array, rows):
    return array.reshape(rows // 8, 8, 32, 128).transpose(0, 2, 1, 3).reshape(rows * 32, 128)


def untiled(array, rows):
    return array.reshape(rows // 8, 32, 8, 128).transpose(0, 2, 1, 3).reshape(1, rows, RANK * RANK)


def body(
    row_bases,
    col_bases,
    row_transfer,
    col_transfer,
    row_order,
    col_order,
    leaf_pattern,
    leaf_blocks,
    root_rows,
    root_cols,
    root_blocks,
):
    vmem, smem, anywhere = pltpu.VMEM, pltpu.SMEM, pl.ANY
    dma = pltpu.SemaphoreType.DMA
    packed = (32, 128)
    scratch = [
        vmem((2, 512, 128), F32),
        vmem((2, 1024, 128), F32),
        vmem((2048, 128), BF16),
        vmem((1024, 128), BF16),
        dma((6,)),
        vmem((2 * 32, RANK, 128), F32),
        vmem((BATCH, RANK, 128), F32),
        vmem((2 * 16, RANK, 128), F32),
        vmem((RANK, RANK, 128), F32),
        vmem((BATCH * RANK, 128), F32),
        vmem((LEAF_DEV, 2 * RANK, RANK), BF16),
        vmem((LEAF_DEV, 2 * RANK, RANK), BF16),
        vmem((N_COL, 2 * RANK, RANK), BF16),
        vmem((N_ROW, 2 * RANK, RANK), BF16),
        vmem((256, 128), F32),
        vmem((2, *packed), F32),
        vmem((2, *packed), F32),
        vmem(packed, F32),
        vmem(packed, F32),
        vmem((N_COL, *packed), F32),
        vmem((N_ROW, *packed), F32),
        dma((N_COL,)),
        dma((N_COL,)),
        dma((N_ROW,)),
        dma((N_ROW,)),
    ]
    for tree in range(2):
        for depth in STAGES[tree]:
            size = 1 << depth
            scratch += [
                vmem((depth, *packed), F32),
                vmem((depth, *packed), F32),
                vmem((size, *packed), F32),
                dma((size,)),
                dma((depth,)),
                dma((size,)),
                dma((size,)),
            ]
    leaf_out, root_out, row_out, col_out = pl.pallas_call(
        kernel,
        out_shape=(
            jax.ShapeDtypeStruct((LEAF_PAIRS * 32, 128), F32),
            jax.ShapeDtypeStruct((ROOT_PAIRS * 32, 128), F32),
            jax.ShapeDtypeStruct(packed, F32),
            jax.ShapeDtypeStruct(packed, F32),
        ),
        in_specs=[pl.BlockSpec(memory_space=smem)] * 5 + [pl.BlockSpec(memory_space=anywhere)] * 6,
        out_specs=(pl.BlockSpec(memory_space=vmem),) * 4,
        scratch_shapes=scratch,
        compiler_params=pltpu.CompilerParams(
            collective_id=0, has_side_effects=True, vmem_limit_bytes=40 * 2**20
        ),
    )(
        row_order.reshape(LEAF_DEV),
        col_order.reshape(LEAF_DEV),
        leaf_pattern.reshape(2 * LEAF_PAIRS),
        root_rows.reshape(ROOT_PAIRS),
        root_cols.reshape(ROOT_PAIRS),
        tiled(row_bases, LEAF_DEV),
        tiled(col_bases, LEAF_DEV),
        tiled(row_transfer, 2 * LEAF_DEV),
        tiled(col_transfer, 2 * LEAF_DEV),
        tiled(leaf_blocks, LEAF_PAIRS),
        tiled(root_blocks, ROOT_PAIRS),
    )
    return (
        untiled(leaf_out, LEAF_PAIRS),
        untiled(root_out, ROOT_PAIRS),
        row_out.reshape(1, 1, RANK * RANK),
        col_out.reshape(1, 1, RANK * RANK),
    )


def solution(mesh):
    return jax.shard_map(
        body,
        mesh=mesh,
        in_specs=(
            P("row", "col", None),
            P("col", "row", None),
            P("row", "col", None),
            P("col", "row", None),
            P("row", "col", None),
            P("col", "row", None),
            P("row", "col", None),
            P("row", "col", None),
            P("row", "col", None),
            P("row", "col", None),
            P("row", "col", None),
        ),
        out_specs=(
            P("row", "col", None),
            P("row", "col", None),
            P("row", "col", None),
            P("col", "row", None),
        ),
        check_vma=False,
    )
```

time: 523 us -> 71.6 us (0.14)
  the two profiles are of different devices: /device:TPU:8 before, /device:TPU:1 now
where the time goes in v1:
time: 71.6 us; the launch traced here: 71.2 us
  Pallas kernels  60.3 us (84%)
  local copies, waits for them, and re-layouts  10.3 us (14%)
    pallas_call x1, Pallas kernels, body(): pl.pallas_call(kernel, out_shape=(jax.ShapeDtypeStruct((LEAF_PAIRS * 32,...  60.3 us
    unnamed x26, local copies, waits for them, and re-layouts  10.2 us

profile of v1, /device:TPU:1, one launch (start us, length us, event | category | flops | bytes accessed | tf_op | source)
XLA Modules:
  0.0 71.2 jit_solution(18110938840838847799)
XLA Ops:
  0.6 0.0 copy-start.10
  0.6 0.0 copy-start.9
  0.7 0.7 copy-done.10
  1.3 0.0 copy-start.6
  1.3 0.0 copy-start.7
  1.3 0.0 copy-start.8
  1.3 0.1 reshape.79.leaf_pattern
  1.4 0.0 copy-done.9
  1.4 0.6 copy-done.6
  2.0 0.0 copy-done.7
  2.0 0.0 copy-done.8
  2.0 0.0 copy-start
  2.0 1.0 %copy-done = f32[1,32,4096]{2,1,0:T(8,128)S(1)} copy-done((f32[1,32,4096]{2,1,0:T(8,128)S(1)}, f32[1,32,4096]{2,1,0:T(8,128)}, u32[]{:S(2)}) %copy-start) | copy-done | bytes 524312
  3.0 0.0 copy-start.1
  3.0 1.0 %copy-done.1 = f32[1,32,4096]{2,1,0:T(8,128)S(1)} copy-done((f32[1,32,4096]{2,1,0:T(8,128)S(1)}, f32[1,32,4096]{2,1,0:T(8,128)}, u32[]{:S(2)}) %copy-start.1) | copy-done | bytes 524312
  4.1 0.0 copy-start.2
  4.1 1.0 %copy-done.2 = bf16[1,64,4096]{2,1,0:T(8,128)(2,1)S(1)} copy-done((bf16[1,64,4096]{2,1,0:T(8,128)(2,1)S(1)}, bf16[1,64,4096]{2,1,0:T(8,128)(2,1)}, u32[]{:S(2)}) %copy-start.2) | copy-done | bytes 524312
  5.1 0.0 copy-start.3
  5.1 0.9 %copy-done.3 = f32[1,16,4096]{2,1,0:T(8,128)S(1)} copy-done((f32[1,16,4096]{2,1,0:T(8,128)S(1)}, f32[1,16,4096]{2,1,0:T(8,128)}, u32[]{:S(2)}) %copy-start.3) | copy-done | bytes 262168
  6.1 0.0 copy-start.4
  6.1 0.9 %copy-done.4 = f32[1,16,4096]{2,1,0:T(8,128)S(1)} copy-done((f32[1,16,4096]{2,1,0:T(8,128)S(1)}, f32[1,16,4096]{2,1,0:T(8,128)}, u32[]{:S(2)}) %copy-start.4) | copy-done | bytes 262168
  7.0 0.0 copy-start.5
  7.0 0.9 %copy-done.5 = bf16[1,32,4096]{2,1,0:T(8,128)(2,1)S(1)} copy-done((bf16[1,32,4096]{2,1,0:T(8,128)(2,1)S(1)}, bf16[1,32,4096]{2,1,0:T(8,128)(2,1)}, u32[]{:S(2)}) %copy-start.5) | copy-done | bytes 262168
  8.0 60.3 %shard_map.138 = (f32[2048,128]{1,0:T(8,128)S(1)}, f32[1024,128]{1,0:T(8,128)S(1)}, f32[32,128]{1,0:T(8,128)S(1)}, f32[32,128]{1,0:T(8,128)S(1)}) custom-call(s32[16]{0:T(128)S(1)} %bitcast.56, s32[16]{0:T(128)S(1)} %bitcast.57, s32[128]{0:T(128)S(1)} %reshape.79.leaf_pattern, s32[32]{0:T(128)S(1)} %bitcast.58, s32[32]{0:T(128)S(1)} %bitcast.59, ...), custom_call_target="tpu_custom_call" | custom-call | tf_op jit(solution)/shard_map/pallas_call | solution.py:600
  68.3 1.0 %copy.19 = f32[1,64,4096]{2,1,0:T(8,128)} copy(f32[1,64,4096]{2,1,0:T(8,128)S(1)} %bitcast.46) | data formatting | bytes 2097152
  69.2 0.8 %copy.20 = f32[1,32,4096]{2,1,0:T(8,128)} copy(f32[1,32,4096]{2,1,0:T(8,128)S(1)} %bitcast.47) | data formatting | bytes 1048576
  70.0 0.6 copy.21
  70.6 0.6 copy.22
Async XLA Ops:
  0.6 0.7 copy-start.10
  0.6 0.8 %copy-start.9 = (s32[1,1,32]{2,1,0:T(1,128)S(1)}, s32[1,1,32]{2,1,0:T(1,128)}, u32[]{:S(2)}) copy-start(s32[1,1,32]{2,1,0:T(1,128)} %param.20) | copy-start | bytes 388
  1.3 0.7 copy-start.6
  1.3 0.7 copy-start.7
  1.3 0.7 copy-start.8
  2.0 1.0 %copy-start = (f32[1,32,4096]{2,1,0:T(8,128)S(1)}, f32[1,32,4096]{2,1,0:T(8,128)}, u32[]{:S(2)}) copy-start(f32[1,32,4096]{2,1,0:T(8,128)} %param.13) | copy-start | bytes 1572868
  3.0 1.0 %copy-start.1 = (f32[1,32,4096]{2,1,0:T(8,128)S(1)}, f32[1,32,4096]{2,1,0:T(8,128)}, u32[]{:S(2)}) copy-start(f32[1,32,4096]{2,1,0:T(8,128)} %param.14) | copy-start | bytes 1572868
  4.1 1.0 %copy-start.2 = (bf16[1,64,4096]{2,1,0:T(8,128)(2,1)S(1)}, bf16[1,64,4096]{2,1,0:T(8,128)(2,1)}, u32[]{:S(2)}) copy-start(bf16[1,64,4096]{2,1,0:T(8,128)(2,1)} %param.18) | copy-start | bytes 1572868
  5.1 0.9 %copy-start.3 = (f32[1,16,4096]{2,1,0:T(8,128)S(1)}, f32[1,16,4096]{2,1,0:T(8,128)}, u32[]{:S(2)}) copy-start(f32[1,16,4096]{2,1,0:T(8,128)} %param.11) | copy-start | bytes 786436
  6.1 0.9 %copy-start.4 = (f32[1,16,4096]{2,1,0:T(8,128)S(1)}, f32[1,16,4096]{2,1,0:T(8,128)}, u32[]{:S(2)}) copy-start(f32[1,16,4096]{2,1,0:T(8,128)} %param.12) | copy-start | bytes 786436
  7.0 0.9 %copy-start.5 = (bf16[1,32,4096]{2,1,0:T(8,128)(2,1)S(1)}, bf16[1,32,4096]{2,1,0:T(8,128)(2,1)}, u32[]{:S(2)}) copy-start(bf16[1,32,4096]{2,1,0:T(8,128)(2,1)} %param.21) | copy-start | bytes 786436

commit v2 on v1

--- a/solution.py
+++ b/solution.py
@@ -174,7 +174,7 @@
 
 
 def to_lanes(gram_ref, batch_ref, count):
-    flat = gram_ref.reshape(BATCH * RANK, 128)
+    flat = gram_ref.reshape(gram_ref.shape[0] * RANK, 128)
 
     def step(j, carry):
         rows = flat[pl.ds(j, count, stride=RANK), :]
@@ -185,43 +185,84 @@
 
 
 def factor(batch_ref):
-    for block in range(8):
-        first = 8 * block
-        columns = [batch_ref[first + c, first:, :] for c in range(8)]
-        for c in range(8):
-            pivot = columns[c][c : c + 1, :]
-            column = columns[c] * lax.rsqrt(pivot)
-            columns[c] = column
-            batch_ref[first + c, first:, :] = column
+    def diagonal(block):
+        first, span = 8 * block, slice(8 * block, 8 * block + 8)
+        columns = [batch_ref[first + c, span, :] for c in range(8)]
+        inverses = []
+
+        def step(c):
+            inverse = lax.rsqrt(jnp.broadcast_to(columns[c][c : c + 1, :], (8, 128)))
+            column = columns[c] * inverse
+            batch_ref[first + c, span, :] = column
+            inverses.append(inverse)
             for later in range(c + 1, 8):
                 columns[later] = columns[later] - column * column[later : later + 1, :]
-        for other in range(block + 1, 8):
-
-            def update(step, carry, first=first, other=other):
-                j = 8 * other + step
-                total = batch_ref[j, 8 * other :, :]
-                for c in range(8):
-                    total = total - batch_ref[first + c, 8 * other :, :] * batch_ref[first + c, pl.ds(j, 1), :]
-                batch_ref[j, 8 * other :, :] = total
-                return carry
-
-            lax.fori_loop(0, 8, update, 0, unroll=4)
+
+        return [functools.partial(step, c) for c in range(8)], inverses
+
+    def below(block, other, inverses):
+        first, span = 8 * block, slice(8 * other, 8 * other + 8)
+        done = []
+        for c in range(8):
+            column = batch_ref[first + c, span, :]
+            for k in range(c):
+                column = column - done[k] * batch_ref[first + k, first + c : first + c + 1, :]
+            column = column * inverses[c]
+            batch_ref[first + c, span, :] = column
+            done.append(column)
+
+    def update(block, j, low, high):
+        first, span = 8 * block, slice(8 * low, 8 * high)
+        total = batch_ref[j, span, :]
+        for c in range(8):
+            total = total - batch_ref[first + c, span, :] * batch_ref[first + c, j : j + 1, :]
+        batch_ref[j, span, :] = total
+
+    steps, inverses = diagonal(0)
+    for step in steps:
+        step()
+    for block in range(7):
+        after = block + 1
+        below(block, after, inverses)
+        for j in range(8 * after, 8 * after + 8):
+            update(block, j, after, after + 1)
+        pieces = [functools.partial(below, block, other, inverses) for other in range(after + 1, 8)]
+        if after < 7:
+            pieces += [functools.partial(update, block, j, after + 1, 8) for j in range(8 * after, 8 * after + 8)]
+        pieces += [functools.partial(update, block, j, j // 8, 8) for j in range(8 * after + 8, RANK)]
+        steps, inverses = diagonal(after)
+        for n, step in enumerate(steps):
+            step()
+            for piece in pieces[n * len(pieces) // 8 : (n + 1) * len(pieces) // 8]:
+                piece()
 
 
 def from_lanes(batch_ref, factor_ref, counts):
-    lane = lax.broadcasted_iota(jnp.int32, (1, 128), 1)
-    column = jnp.where(lane < 32, 2 * lane, jnp.where(lane < 64, 2 * lane - 63, lane - 64))
+    place = lax.broadcasted_iota(jnp.int32, (RANK, 128), 0)
+    first_group = lax.broadcasted_iota(jnp.int32, (RANK, 128), 1) < counts[0]
+    halved = jnp.where(place < 32, 2 * place, 2 * place - 63)
+    column = jnp.where(first_group, halved, place)
 
     def step(j, carry):
         plane = batch_ref.at[j]
-        values = jnp.concatenate(
-            [plane[pl.ds(0, 32, stride=2), :], plane[pl.ds(1, 32, stride=2), :], plane[...]], 0
-        ).T
-        values = jnp.where(column >= j, values[: sum(counts)], 0.0)
+        halves = jnp.concatenate([plane[pl.ds(0, 32, stride=2), :], plane[pl.ds(1, 32, stride=2), :]], 0)
+        values = jnp.where(first_group, halves, plane[...])
+        values = jnp.where(column >= j, values, 0.0).T
         moved = lax.div(j, 2) + 32 * lax.rem(j, 2)
-        factor_ref[pl.ds(moved, counts[0], stride=RANK), :] = values[: counts[0]]
-        if len(counts) > 1:
-            factor_ref[pl.ds(counts[0] * RANK + j, counts[1], stride=RANK), :] = values[counts[0] :]
+        factor_ref[pl.ds(moved, counts[0], stride=RANK), :RANK] = values[: counts[0]]
+        factor_ref[pl.ds(counts[0] * RANK + j, counts[1], stride=RANK), :RANK] = values[counts[0] : sum(counts)]
+        return carry
+
+    lax.fori_loop(0, RANK, step, 0, unroll=4)
+
+
+def upper_from_lanes(batch_ref, factor_ref):
+    place = lax.broadcasted_iota(jnp.int32, (RANK, 128), 0)
+
+    def step(j, carry):
+        values = jnp.where(place >= j, batch_ref[j], 0.0).T
+        moved = lax.div(j, 2) + 32 * lax.rem(j, 2)
+        factor_ref[pl.ds(moved, 8, stride=RANK), :RANK] = values[:8]
         return carry
 
     lax.fori_loop(0, RANK, step, 0, unroll=4)
@@ -254,25 +295,26 @@
 
 
 def kernel(
-    row_order,
-    col_order,
-    leaf_pattern,
-    root_rows,
-    root_cols,
+    row_order_hbm,
+    col_order_hbm,
+    leaf_pattern_hbm,
     row_bases_hbm,
     col_bases_hbm,
     row_transfer_hbm,
     col_transfer_hbm,
     leaf_blocks_hbm,
-    root_blocks_hbm,
+    leaf_hbm,
+    highest_hbm,
+    row_table,
+    col_table,
     leaf_out,
-    root_out,
-    row_out,
-    col_out,
+    stores,
+    row_order,
+    col_order,
+    leaf_pattern,
     bases,
     transfers,
     leaf_blocks,
-    root_blocks,
     loads,
     natural,
     grams,
@@ -281,15 +323,11 @@
     factors,
     leaf_left,
     leaf_right,
-    root_left,
-    root_right,
     block_stage,
     inner_own,
     highest,
     row_own,
     col_own,
-    row_table,
-    col_table,
     row_sent,
     row_got,
     col_sent,
@@ -302,17 +340,30 @@
         pltpu.make_async_copy(source, target, loads.at[n])
         for n, (source, target) in enumerate(
             [
+                (row_transfer_hbm, transfers.at[0]),
+                (col_transfer_hbm, transfers.at[1]),
                 (row_bases_hbm, bases.at[0]),
                 (col_bases_hbm, bases.at[1]),
-                (row_transfer_hbm, transfers.at[0]),
-                (col_transfer_hbm, transfers.at[1]),
+                (row_order_hbm, row_order),
+                (col_order_hbm, col_order),
                 (leaf_blocks_hbm, leaf_blocks),
-                (root_blocks_hbm, root_blocks),
+                (leaf_pattern_hbm, leaf_pattern),
             ]
         )
     ]
     for copy in copies:
         copy.start()
+    leaf_store, highest_store, row_keep, col_keep = (
+        pltpu.make_async_copy(source, target, stores.at[n])
+        for n, (source, target) in enumerate(
+            [
+                (leaf_out, leaf_hbm),
+                (highest, highest_hbm),
+                (row_own, row_table.at[place_col]),
+                (col_own, col_table.at[place_row]),
+            ]
+        )
+    )
     barrier = pltpu.get_barrier_semaphore()
 
     def greet(axis, size, place):
@@ -352,8 +403,8 @@
             at = 7 * (3 * tree + n)
             stages[tree].append(Stage(STAGES[tree][n], *layout[tree][n], stage_refs[at : at + 7]))
 
-    copies[2].wait()
-    copies[3].wait()
+    for copy in copies[:2]:
+        copy.wait()
     for tree in range(2):
 
         def lay_out(m, carry, tree=tree):
@@ -375,8 +426,8 @@
         for n in range(3):
             stages[tree][n].send_inner(inner_own.at[tree])
 
-    copies[0].wait()
-    copies[1].wait()
+    for copy in copies[2:6]:
+        copy.wait()
 
     def leaf_gram(leaf, carry):
         for tree in range(2):
@@ -393,7 +444,7 @@
         for tree in range(2):
             total = None
             for child in range(2):
-                leaf = orders[tree][2 * q + child]
+                leaf = orders[tree][0, 0, 2 * q + child]
                 term = sandwich(grams[tree * GROUP + leaf][:, :RANK], transfer_of(tree, leaf))
                 total = term if total is None else total + term
             nodes[tree * 16 + q, :, :RANK] = total
@@ -428,9 +479,9 @@
     factor(batch)
     from_lanes(batch, factors, (GROUP, GROUP))
     row_own[...] = pack(factors[LEAF_DEV * RANK : (LEAF_DEV + 1) * RANK, :RANK])
-    col_own[...] = pack(factors[(GROUP + LEAF_DEV) * RANK : (GROUP + LEAF_DEV + 1) * RANK, RANK:])
-    row_table[place_col] = row_own[...]
-    col_table[place_row] = col_own[...]
+    col_own[...] = pack(factors[(GROUP + LEAF_DEV) * RANK : (GROUP + LEAF_DEV + 1) * RANK, :RANK])
+    row_keep.start()
+    col_keep.start()
 
     def table_copy(axis, size, place, own, table, sent, got, k, slot):
         return pltpu.make_async_remote_copy(
@@ -454,7 +505,7 @@
 
     for leaf in range(LEAF_DEV):
         leaf_left[leaf] = table_entry(factors[leaf * RANK : (leaf + 1) * RANK, :RANK])
-        leaf_right[leaf] = table_entry(factors[(GROUP + leaf) * RANK : (GROUP + leaf + 1) * RANK, RANK:])
+        leaf_right[leaf] = table_entry(factors[(GROUP + leaf) * RANK : (GROUP + leaf + 1) * RANK, :RANK])
 
     def climb(n):
         for tree in range(2):
@@ -470,19 +521,24 @@
             stage.send_terms()
 
     climb(1)
-    copies[4].wait()
+    for copy in copies[6:8]:
+        copy.wait()
     couple(
         LEAF_PAIRS,
         leaf_blocks,
         block_stage,
         leaf_left,
         leaf_right,
-        lambda pair: leaf_pattern[pair],
-        lambda pair: leaf_pattern[LEAF_PAIRS + pair],
+        lambda pair: leaf_pattern[0, 0, pair],
+        lambda pair: leaf_pattern[0, 1, pair],
         leaf_out,
     )
+    leaf_store.start()
     climb(2)
 
+    for tree in range(2):
+        stages[tree][2].receive_terms(highest.at[tree])
+    highest_store.start()
     for parts in (row_parts, col_parts):
 
         def receive(k, carry, parts=parts):
@@ -492,6 +548,89 @@
 
         lax.fori_loop(1, parts[1], receive, 0)
 
+    for tree in range(2):
+        for n in range(3):
+            stages[tree][n].finish()
+    for parts in (row_parts, col_parts):
+
+        def drain(k, carry, parts=parts):
+            table_copy(*parts, k, parts[2]).wait_send()
+            return carry
+
+        lax.fori_loop(1, parts[1], drain, 0)
+    for store in (leaf_store, highest_store, row_keep, col_keep):
+        store.wait()
+
+
+def finish(
+    leaf_hbm,
+    highest_hbm,
+    row_table_hbm,
+    col_table_hbm,
+    root_rows_hbm,
+    root_cols_hbm,
+    root_blocks_hbm,
+    leaf_end,
+    root_end,
+    row_end,
+    col_end,
+    leaf_pass,
+    highest,
+    row_table,
+    col_table,
+    root_rows,
+    root_cols,
+    root_blocks,
+    root_out,
+    row_out,
+    col_out,
+    loads,
+    stores,
+    grams,
+    batch,
+    factors,
+    root_left,
+    root_right,
+    block_stage,
+):
+    copies = [
+        pltpu.make_async_copy(source, target, loads.at[n])
+        for n, (source, target) in enumerate(
+            [
+                (highest_hbm, highest),
+                (leaf_hbm, leaf_pass),
+                (row_table_hbm, row_table),
+                (col_table_hbm, col_table),
+                (root_rows_hbm, root_rows),
+                (root_cols_hbm, root_cols),
+                (root_blocks_hbm, root_blocks),
+            ]
+        )
+    ]
+    for copy in copies:
+        copy.start()
+    results = [
+        pltpu.make_async_copy(source, target, stores.at[n])
+        for n, (source, target) in enumerate(
+            [(leaf_pass, leaf_end), (row_out, row_end), (col_out, col_end), (root_out, root_end)]
+        )
+    ]
+    copies[0].wait()
+    for tree in range(2):
+        grams[tree, :, :RANK] = unpack(highest[tree])
+    to_lanes(grams, batch, 8)
+    factor(batch)
+    copies[1].wait()
+    results[0].start()
+    upper_from_lanes(batch, factors)
+    for tree, out in enumerate((row_out, col_out)):
+        out[...] = pack(factors[tree * RANK : (tree + 1) * RANK, :RANK])
+    results[1].start()
+    results[2].start()
+
+    for copy in copies[2:]:
+        copy.wait()
+
     def convert(table, entries, count):
         def step(n, carry):
             entries[n] = table_entry(unpack(table[n]))
@@ -501,37 +640,19 @@
 
     convert(row_table, root_left, N_COL)
     convert(col_table, root_right, N_ROW)
-    copies[5].wait()
     couple(
         ROOT_PAIRS,
         root_blocks,
         block_stage,
         root_left,
         root_right,
-        lambda pair: root_rows[pair],
-        lambda pair: root_cols[pair],
+        lambda pair: root_rows[0, 0, pair],
+        lambda pair: root_cols[0, 0, pair],
         root_out,
     )
-
-    for tree in range(2):
-        stages[tree][2].receive_terms(highest.at[tree])
-        grams[tree, :, :RANK] = unpack(highest[tree])
-    to_lanes(grams, batch, 8)
-    factor(batch)
-    from_lanes(batch, factors, (8,))
-    for tree, out in enumerate((row_out, col_out)):
-        out[...] = pack(factors[tree * RANK : (tree + 1) * RANK, RANK:])
-
-    for tree in range(2):
-        for n in range(3):
-            stages[tree][n].finish()
-    for parts in (row_parts, col_parts):
-
-        def drain(k, carry, parts=parts):
-            table_copy(*parts, k, parts[2]).wait_send()
-            return carry
-
-        lax.fori_loop(1, parts[1], drain, 0)
+    results[3].start()
+    for result in results:
+        result.wait()
 
 
 def tiled(array, rows):
@@ -555,15 +676,21 @@
     root_cols,
     root_blocks,
 ):
-    vmem, smem, anywhere = pltpu.VMEM, pltpu.SMEM, pl.ANY
+    vmem, smem = pltpu.VMEM, pltpu.SMEM
     dma = pltpu.SemaphoreType.DMA
+    hbm = pl.BlockSpec(memory_space=pltpu.HBM)
+    shape = jax.ShapeDtypeStruct
     packed = (32, 128)
     scratch = [
+        vmem((LEAF_PAIRS * 32, 128), F32),
+        dma((4,)),
+        smem((1, 1, LEAF_DEV), jnp.int32),
+        smem((1, 1, LEAF_DEV), jnp.int32),
+        smem((1, 2, LEAF_PAIRS), jnp.int32),
         vmem((2, 512, 128), F32),
         vmem((2, 1024, 128), F32),
         vmem((2048, 128), BF16),
-        vmem((1024, 128), BF16),
-        dma((6,)),
+        dma((8,)),
         vmem((2 * 32, RANK, 128), F32),
         vmem((BATCH, RANK, 128), F32),
         vmem((2 * 16, RANK, 128), F32),
@@ -571,15 +698,11 @@
         vmem((BATCH * RANK, 128), F32),
         vmem((LEAF_DEV, 2 * RANK, RANK), BF16),
         vmem((LEAF_DEV, 2 * RANK, RANK), BF16),
-        vmem((N_COL, 2 * RANK, RANK), BF16),
-        vmem((N_ROW, 2 * RANK, RANK), BF16),
         vmem((256, 128), F32),
         vmem((2, *packed), F32),
         vmem((2, *packed), F32),
         vmem(packed, F32),
         vmem(packed, F32),
-        vmem((N_COL, *packed), F32),
-        vmem((N_ROW, *packed), F32),
         dma((N_COL,)),
         dma((N_COL,)),
         dma((N_ROW,)),
@@ -597,33 +720,62 @@
                 dma((size,)),
                 dma((size,)),
             ]
-    leaf_out, root_out, row_out, col_out = pl.pallas_call(
+    parts = pl.pallas_call(
         kernel,
         out_shape=(
-            jax.ShapeDtypeStruct((LEAF_PAIRS * 32, 128), F32),
-            jax.ShapeDtypeStruct((ROOT_PAIRS * 32, 128), F32),
-            jax.ShapeDtypeStruct(packed, F32),
-            jax.ShapeDtypeStruct(packed, F32),
+            shape((LEAF_PAIRS * 32, 128), F32),
+            shape((2, *packed), F32),
+            shape((N_COL, *packed), F32),
+            shape((N_ROW, *packed), F32),
         ),
-        in_specs=[pl.BlockSpec(memory_space=smem)] * 5 + [pl.BlockSpec(memory_space=anywhere)] * 6,
-        out_specs=(pl.BlockSpec(memory_space=vmem),) * 4,
+        in_specs=[hbm] * 8,
+        out_specs=(hbm,) * 4,
         scratch_shapes=scratch,
         compiler_params=pltpu.CompilerParams(
-            collective_id=0, has_side_effects=True, vmem_limit_bytes=40 * 2**20
+            collective_id=0, has_side_effects=True, vmem_limit_bytes=62 * 2**20
         ),
     )(
-        row_order.reshape(LEAF_DEV),
-        col_order.reshape(LEAF_DEV),
-        leaf_pattern.reshape(2 * LEAF_PAIRS),
-        root_rows.reshape(ROOT_PAIRS),
-        root_cols.reshape(ROOT_PAIRS),
+        row_order,
+        col_order,
+        leaf_pattern,
         tiled(row_bases, LEAF_DEV),
         tiled(col_bases, LEAF_DEV),
         tiled(row_transfer, 2 * LEAF_DEV),
         tiled(col_transfer, 2 * LEAF_DEV),
         tiled(leaf_blocks, LEAF_PAIRS),
-        tiled(root_blocks, ROOT_PAIRS),
     )
+    leaf_out, root_out, row_out, col_out = pl.pallas_call(
+        finish,
+        out_shape=(
+            shape((LEAF_PAIRS * 32, 128), F32),
+            shape((ROOT_PAIRS * 32, 128), F32),
+            shape(packed, F32),
+            shape(packed, F32),
+        ),
+        in_specs=[hbm] * 7,
+        out_specs=(hbm,) * 4,
+        scratch_shapes=[
+            vmem((LEAF_PAIRS * 32, 128), F32),
+            vmem((2, *packed), F32),
+            vmem((N_COL, *packed), F32),
+            vmem((N_ROW, *packed), F32),
+            smem((1, 1, ROOT_PAIRS), jnp.int32),
+            smem((1, 1, ROOT_PAIRS), jnp.int32),
+            vmem((1024, 128), BF16),
+            vmem((ROOT_PAIRS * 32, 128), F32),
+            vmem(packed, F32),
+            vmem(packed, F32),
+            dma((7,)),
+            dma((4,)),
+            vmem((8, RANK, 128), F32),
+            vmem((RANK, RANK, 128), F32),
+            vmem((8 * RANK, 128), F32),
+            vmem((N_COL, 2 * RANK, RANK), BF16),
+            vmem((N_ROW, 2 * RANK, RANK), BF16),
+            vmem((256, 128), F32),
+        ],
+        compiler_params=pltpu.CompilerParams(vmem_limit_bytes=62 * 2**20),
+    )(*parts, root_rows, root_cols, tiled(root_blocks, ROOT_PAIRS))
     return (
         untiled(leaf_out, LEAF_PAIRS),
         untiled(root_out, ROOT_PAIRS),

time: 71.6 us -> 61.8 us (0.86)
  the two profiles are of different devices: /device:TPU:1 before, /device:TPU:16 now
where the time goes in v2:
time: 61.8 us; the launch traced here: 61.6 us
  Pallas kernels  61 us (99%)
  between operations  0.64 us (1%)
    pallas_call x1, Pallas kernels, body(): pl.pallas_call(kernel, out_shape=(shape((LEAF_PAIRS * 32, 128), F32), sha...  49.7 us
    pallas_call x1, Pallas kernels, body(): pl.pallas_call(finish, out_shape=(shape((LEAF_PAIRS * 32, 128), F32), sha...  11.2 us

profile of v2, /device:TPU:16, one launch (start us, length us, event | category | flops | bytes accessed | tf_op | source)
XLA Modules:
  0.0 61.6 jit_solution(11475532266848402996)
XLA Ops:
  0.6 49.7 %shard_map.138 = (f32[2048,128]{1,0:T(8,128)}, f32[2,32,128]{2,1,0:T(8,128)}, f32[32,32,128]{2,1,0:T(8,128)}, f32[16,32,128]{2,1,0:T(8,128)}) custom-call(s32[1,1,16]{2,1,0:T(1,128)} %row_order_hbm.1, s32[1,1,16]{2,1,0:T(1,128)} %col_order_hbm.1, s32[1,2,64]{2,1,0:T(2,128)} %leaf_pattern_hbm.1, f32[512,128]{1,0:T(8,128)} %bitcast.45, f32[512,128]{1,0:T(8,128)} %bitcast.46, ...), custom_call_target="tpu_custom_call" | custom-call | tf_op jit(solution)/shard_map/pallas_call | solution.py:723
  50.4 11.2 %shard_map.139 = (f32[2048,128]{1,0:T(8,128)}, f32[1024,128]{1,0:T(8,128)}, f32[32,128]{1,0:T(8,128)}, f32[32,128]{1,0:T(8,128)}) custom-call(f32[2048,128]{1,0:T(8,128)} %get-tuple-element.12.leaf_hbm, f32[2,32,128]{2,1,0:T(8,128)} %get-tuple-element.13.highest_hbm, f32[32,32,128]{2,1,0:T(8,128)} %get-tuple-element.14.row_table_hbm, ...), custom_call_target="tpu_custom_call" | custom-call | tf_op jit(solution)/shard_map/pallas_call | solution.py:747

commit v3 on v2

--- a/solution.py
+++ b/solution.py
@@ -15,8 +15,9 @@
 N_COL = 32
 N_X = 4
 N_Y = 8
-GROUP = 24
-BATCH = 2 * GROUP
+N_Z = 8
+N_CORE = 2
+ROOT_BATCH = N_COL + N_ROW + 8
 MESH = pl.DeviceIdType.MESH
 F32 = jnp.float32
 BF16 = jnp.bfloat16
@@ -251,18 +252,6 @@
         moved = lax.div(j, 2) + 32 * lax.rem(j, 2)
         factor_ref[pl.ds(moved, counts[0], stride=RANK), :RANK] = values[: counts[0]]
         factor_ref[pl.ds(counts[0] * RANK + j, counts[1], stride=RANK), :RANK] = values[counts[0] : sum(counts)]
-        return carry
-
-    lax.fori_loop(0, RANK, step, 0, unroll=4)
-
-
-def upper_from_lanes(batch_ref, factor_ref):
-    place = lax.broadcasted_iota(jnp.int32, (RANK, 128), 0)
-
-    def step(j, carry):
-        values = jnp.where(place >= j, batch_ref[j], 0.0).T
-        moved = lax.div(j, 2) + 32 * lax.rem(j, 2)
-        factor_ref[pl.ds(moved, 8, stride=RANK), :RANK] = values[:8]
         return carry
 
     lax.fori_loop(0, RANK, step, 0, unroll=4)
@@ -326,12 +315,13 @@
     block_stage,
     inner_own,
     highest,
-    row_own,
-    col_own,
-    row_sent,
-    row_got,
-    col_sent,
-    col_got,
+    roots,
+    root_own,
+    root_line,
+    line_sent,
+    line_got,
+    spread_sent,
+    spread_got,
     *stage_refs,
 ):
     place_row = lax.axis_index("row")
@@ -353,17 +343,8 @@
     ]
     for copy in copies:
         copy.start()
-    leaf_store, highest_store, row_keep, col_keep = (
-        pltpu.make_async_copy(source, target, stores.at[n])
-        for n, (source, target) in enumerate(
-            [
-                (leaf_out, leaf_hbm),
-                (highest, highest_hbm),
-                (row_own, row_table.at[place_col]),
-                (col_own, col_table.at[place_row]),
-            ]
-        )
-    )
+    leaf_store = pltpu.make_async_copy(leaf_out, leaf_hbm, stores.at[0])
+    highest_store = pltpu.make_async_copy(highest, highest_hbm, stores.at[1])
     barrier = pltpu.get_barrier_semaphore()
 
     def greet(axis, size, place):
@@ -384,6 +365,42 @@
     x_peer = lambda p: {"col": y_place * N_X + p}
     y_peer = lambda p: {"col": p * N_X}
     z_peer = lambda p: {"row": jnp.int32(p)}
+    z_place = lax.div(place_row, N_CORE)
+    core_place = lax.rem(place_row, N_CORE)
+    line_places = (y_place, z_place)
+
+    def line_copy(tree, k, slot):
+        place = lax.rem(line_places[tree] + k, 8)
+        peer = {"col": place * N_X + x_place} if tree == 0 else {"row": place * N_CORE + core_place}
+        return pltpu.make_async_remote_copy(
+            root_own.at[tree],
+            root_line.at[tree, slot],
+            line_sent.at[tree, k],
+            line_got.at[tree, slot],
+            device_id=peer,
+            device_id_type=MESH,
+        )
+
+    spreads = ((row_table, N_X, x_place), (col_table, N_CORE, core_place))
+
+    def spread_copy(tree, k, slot):
+        table, size, place = spreads[tree]
+        to = lax.rem(place + k, size)
+        peer = {"col": y_place * N_X + to} if tree == 0 else {"row": z_place * N_CORE + to}
+        return pltpu.make_async_remote_copy(
+            root_line.at[tree],
+            table.at[slot],
+            spread_sent.at[tree, k],
+            spread_got.at[tree, slot],
+            device_id=peer,
+            device_id_type=MESH,
+        )
+
+    spread_copies = [[spread_copy(tree, k, spreads[tree][2]) for k in range(1, spreads[tree][1])] for tree in range(2)]
+    keep_copies = [
+        pltpu.make_async_copy(root_line.at[tree], spreads[tree][0].at[spreads[tree][2]], stores.at[2 + tree])
+        for tree in range(2)
+    ]
     layout = (
         (
             (x_place, always, x_peer),
@@ -433,7 +450,7 @@
         for tree in range(2):
             rows = bases[tree, pl.ds(lax.div(leaf, 8) * 256 + lax.rem(leaf, 8), 32, stride=8), :]
             basis = unpack(rows)
-            grams[tree * GROUP + leaf, :, :RANK] = product_tn(basis, basis)
+            grams[tree * LEAF_DEV + leaf, :, :RANK] = product_tn(basis, basis)
         return carry
 
     lax.fori_loop(0, LEAF_DEV, leaf_gram, 0, unroll=4)
@@ -445,7 +462,7 @@
             total = None
             for child in range(2):
                 leaf = orders[tree][0, 0, 2 * q + child]
-                term = sandwich(grams[tree * GROUP + leaf][:, :RANK], transfer_of(tree, leaf))
+                term = sandwich(grams[tree * LEAF_DEV + leaf][:, :RANK], transfer_of(tree, leaf))
                 total = term if total is None else total + term
             nodes[tree * 16 + q, :, :RANK] = total
         return carry
@@ -465,47 +482,34 @@
                 if count > 2:
                     nodes[tree * 16 + target + q, :, :RANK] = total
                 else:
-                    grams[tree * GROUP + LEAF_DEV, :, :RANK] = total
+                    roots[tree] = total
         offset += count
         source, target, count = target, target + count // 2, count // 2
 
     for tree in range(2):
         stage = stages[tree][0]
         stage.receive_inner()
-        stage.make_terms(grams[tree * GROUP + LEAF_DEV][:, :RANK], transfer_of(tree, 30))
+        stage.make_terms(roots[tree], transfer_of(tree, 30))
         stage.send_terms()
 
-    to_lanes(grams, batch, BATCH)
+    for tree in range(2):
+        root_own[tree] = pack(roots[tree])
+        root_line[tree, line_places[tree]] = root_own[tree]
+    for tree in range(2):
+        for k in range(1, 8):
+            line_copy(tree, k, line_places[tree]).start()
+
+    to_lanes(grams, batch, 2 * LEAF_DEV)
     factor(batch)
-    from_lanes(batch, factors, (GROUP, GROUP))
-    row_own[...] = pack(factors[LEAF_DEV * RANK : (LEAF_DEV + 1) * RANK, :RANK])
-    col_own[...] = pack(factors[(GROUP + LEAF_DEV) * RANK : (GROUP + LEAF_DEV + 1) * RANK, :RANK])
-    row_keep.start()
-    col_keep.start()
-
-    def table_copy(axis, size, place, own, table, sent, got, k, slot):
-        return pltpu.make_async_remote_copy(
-            own,
-            table.at[slot],
-            sent.at[k],
-            got.at[slot],
-            device_id={axis: lax.rem(place + k, size)},
-            device_id_type=MESH,
-        )
-
-    row_parts = ("col", N_COL, place_col, row_own, row_table, row_sent, row_got)
-    col_parts = ("row", N_ROW, place_row, col_own, col_table, col_sent, col_got)
-    for parts in (row_parts, col_parts):
-
-        def send(k, carry, parts=parts):
-            table_copy(*parts, k, parts[2]).start()
-            return carry
-
-        lax.fori_loop(1, parts[1], send, 0)
-
+    from_lanes(batch, factors, (LEAF_DEV, LEAF_DEV))
+    for tree in range(2):
+        for k in range(1, 8):
+            line_copy(tree, k, lax.rem(line_places[tree] + 8 - k, 8)).wait_recv()
+        for copy in keep_copies[tree : tree + 1] + spread_copies[tree]:
+            copy.start()
     for leaf in range(LEAF_DEV):
         leaf_left[leaf] = table_entry(factors[leaf * RANK : (leaf + 1) * RANK, :RANK])
-        leaf_right[leaf] = table_entry(factors[(GROUP + leaf) * RANK : (GROUP + leaf + 1) * RANK, :RANK])
+        leaf_right[leaf] = table_entry(factors[(LEAF_DEV + leaf) * RANK : (LEAF_DEV + leaf + 1) * RANK, :RANK])
 
     def climb(n):
         for tree in range(2):
@@ -539,26 +543,18 @@
     for tree in range(2):
         stages[tree][2].receive_terms(highest.at[tree])
     highest_store.start()
-    for parts in (row_parts, col_parts):
-
-        def receive(k, carry, parts=parts):
-            size, place = parts[1], parts[2]
-            table_copy(*parts, k, lax.rem(place + size - k, size)).wait_recv()
-            return carry
-
-        lax.fori_loop(1, parts[1], receive, 0)
-
+    for tree in range(2):
+        for k in range(1, spreads[tree][1]):
+            spread_copy(tree, k, lax.rem(spreads[tree][2] + spreads[tree][1] - k, spreads[tree][1])).wait_recv()
     for tree in range(2):
         for n in range(3):
             stages[tree][n].finish()
-    for parts in (row_parts, col_parts):
-
-        def drain(k, carry, parts=parts):
-            table_copy(*parts, k, parts[2]).wait_send()
-            return carry
-
-        lax.fori_loop(1, parts[1], drain, 0)
-    for store in (leaf_store, highest_store, row_keep, col_keep):
+    for tree in range(2):
+        for k in range(1, 8):
+            line_copy(tree, k, line_places[tree]).wait_send()
+        for copy in spread_copies[tree]:
+            copy.wait_send()
+    for store in (leaf_store, highest_store, *keep_copies):
         store.wait()
 
 
@@ -616,38 +612,50 @@
         )
     ]
     copies[0].wait()
-    for tree in range(2):
-        grams[tree, :, :RANK] = unpack(highest[tree])
-    to_lanes(grams, batch, 8)
+    copies[2].wait()
+    copies[3].wait()
+    for tree in range(2):
+        grams[N_COL + N_ROW + tree, :, :RANK] = unpack(highest[tree])
+
+    def spread_out(n, carry):
+        for line in range(4):
+            grams[line * 8 + n, :, :RANK] = unpack(row_table[line, n])
+        for line in range(2):
+            grams[N_COL + line * 8 + n, :, :RANK] = unpack(col_table[line, n])
+        return carry
+
+    lax.fori_loop(0, 8, spread_out, 0, unroll=2)
+    to_lanes(grams, batch, ROOT_BATCH)
     factor(batch)
     copies[1].wait()
     results[0].start()
-    upper_from_lanes(batch, factors)
+    from_lanes(batch, factors, (N_COL, N_ROW + 8))
     for tree, out in enumerate((row_out, col_out)):
-        out[...] = pack(factors[tree * RANK : (tree + 1) * RANK, :RANK])
+        base = (N_COL + N_ROW + tree) * RANK
+        even, odd = (factors[pl.ds(base + half, 32, stride=2), :][:, :RANK] for half in range(2))
+        out[...] = jnp.concatenate([even, odd], 1)
     results[1].start()
     results[2].start()
-
-    for copy in copies[2:]:
+    for copy in copies[4:]:
         copy.wait()
 
-    def convert(table, entries, count):
+    def convert(first, entries, count):
         def step(n, carry):
-            entries[n] = table_entry(unpack(table[n]))
+            entries[n] = table_entry(factors[pl.ds(pl.multiple_of((first + n) * RANK, RANK), RANK), :][:, :RANK])
             return carry
 
         lax.fori_loop(0, count, step, 0, unroll=4)
 
-    convert(row_table, root_left, N_COL)
-    convert(col_table, root_right, N_ROW)
+    convert(0, root_left, N_COL)
+    convert(N_COL, root_right, N_ROW)
     couple(
         ROOT_PAIRS,
         root_blocks,
         block_stage,
         root_left,
         root_right,
-        lambda pair: root_rows[0, 0, pair],
-        lambda pair: root_cols[0, 0, pair],
+        lambda pair: lax.rem(root_rows[0, 0, pair], N_X) * 8 + lax.div(root_rows[0, 0, pair], N_X),
+        lambda pair: lax.rem(root_cols[0, 0, pair], N_CORE) * 8 + lax.div(root_cols[0, 0, pair], N_CORE),
         root_out,
     )
     results[3].start()
@@ -692,21 +700,22 @@
         vmem((2048, 128), BF16),
         dma((8,)),
         vmem((2 * 32, RANK, 128), F32),
-        vmem((BATCH, RANK, 128), F32),
+        vmem((2 * LEAF_DEV, RANK, 128), F32),
         vmem((2 * 16, RANK, 128), F32),
         vmem((RANK, RANK, 128), F32),
-        vmem((BATCH * RANK, 128), F32),
+        vmem((2 * LEAF_DEV * RANK, 128), F32),
         vmem((LEAF_DEV, 2 * RANK, RANK), BF16),
         vmem((LEAF_DEV, 2 * RANK, RANK), BF16),
         vmem((256, 128), F32),
         vmem((2, *packed), F32),
         vmem((2, *packed), F32),
-        vmem(packed, F32),
-        vmem(packed, F32),
-        dma((N_COL,)),
-        dma((N_COL,)),
-        dma((N_ROW,)),
-        dma((N_ROW,)),
+        vmem((2, RANK, RANK), F32),
+        vmem((2, *packed), F32),
+        vmem((2, 8, *packed), F32),
+        dma((2, 8)),
+        dma((2, 8)),
+        dma((2, N_X)),
+        dma((2, N_X)),
     ]
     for tree in range(2):
         for depth in STAGES[tree]:
@@ -725,8 +734,8 @@
         out_shape=(
             shape((LEAF_PAIRS * 32, 128), F32),
             shape((2, *packed), F32),
-            shape((N_COL, *packed), F32),
-            shape((N_ROW, *packed), F32),
+            shape((N_X, N_Y, *packed), F32),
+            shape((N_CORE, N_Z, *packed), F32),
         ),
         in_specs=[hbm] * 8,
         out_specs=(hbm,) * 4,
@@ -757,8 +766,8 @@
         scratch_shapes=[
             vmem((LEAF_PAIRS * 32, 128), F32),
             vmem((2, *packed), F32),
-            vmem((N_COL, *packed), F32),
-            vmem((N_ROW, *packed), F32),
+            vmem((N_X, N_Y, *packed), F32),
+            vmem((N_CORE, N_Z, *packed), F32),
             smem((1, 1, ROOT_PAIRS), jnp.int32),
             smem((1, 1, ROOT_PAIRS), jnp.int32),
             vmem((1024, 128), BF16),
@@ -767,9 +776,9 @@
             vmem(packed, F32),
             dma((7,)),
             dma((4,)),
-            vmem((8, RANK, 128), F32),
+            vmem((ROOT_BATCH, RANK, 128), F32),
             vmem((RANK, RANK, 128), F32),
-            vmem((8 * RANK, 128), F32),
+            vmem((ROOT_BATCH * RANK, 128), F32),
             vmem((N_COL, 2 * RANK, RANK), BF16),
             vmem((N_ROW, 2 * RANK, RANK), BF16),
             vmem((256, 128), F32),

time: 61.8 us -> 61 us (0.987)
  the two profiles are of different devices: /device:TPU:16 before, /device:TPU:32 now
where the time goes in v3:
time: 61 us; the launch traced here: 60.8 us
  Pallas kernels  60.2 us (99%)
  between operations  0.64 us (1%)
    pallas_call x1, Pallas kernels, body(): pl.pallas_call(kernel, out_shape=(shape((LEAF_PAIRS * 32, 128), F32), sha...  46.7 us
    pallas_call x1, Pallas kernels, body(): pl.pallas_call(finish, out_shape=(shape((LEAF_PAIRS * 32, 128), F32), sha...  13.5 us

profile of v3, /device:TPU:32, one launch (start us, length us, event | category | flops | bytes accessed | tf_op | source)
XLA Modules:
  0.0 60.8 jit_solution(6568753024877981798)
XLA Ops:
  0.6 46.7 %shard_map.138 = (f32[2048,128]{1,0:T(8,128)}, f32[2,32,128]{2,1,0:T(8,128)}, f32[4,8,32,128]{3,2,1,0:T(8,128)}, f32[2,8,32,128]{3,2,1,0:T(8,128)}) custom-call(s32[1,1,16]{2,1,0:T(1,128)} %row_order_hbm.1, s32[1,1,16]{2,1,0:T(1,128)} %col_order_hbm.1, s32[1,2,64]{2,1,0:T(2,128)} %leaf_pattern_hbm.1, f32[512,128]{1,0:T(8,128)} %bitcast.45, ...), custom_call_target="tpu_custom_call" | custom-call | tf_op jit(solution)/shard_map/pallas_call | solution.py:732
  47.4 13.5 %shard_map.139 = (f32[2048,128]{1,0:T(8,128)}, f32[1024,128]{1,0:T(8,128)}, f32[32,128]{1,0:T(8,128)}, f32[32,128]{1,0:T(8,128)}) custom-call(f32[2048,128]{1,0:T(8,128)} %get-tuple-element.12.leaf_hbm, f32[2,32,128]{2,1,0:T(8,128)} %get-tuple-element.13.highest_hbm, f32[4,8,32,128]{3,2,1,0:T(8,128)} %get-tuple-element.14.row_table_hbm, ...), custom_call_target="tpu_custom_call" | custom-call | tf_op jit(solution)/shard_map/pallas_call | solution.py:756

commit v4 on v3

--- a/solution.py
+++ b/solution.py
@@ -34,23 +34,16 @@
     )
 
 
-def product_tn(left, right):
-    left_high, left_low = split(left)
-    right_high, right_low = split(right)
-    return contract(
-        jnp.concatenate([left_high, left_high, left_low], 0),
-        jnp.concatenate([right_high, right_low, right_high], 0),
-        0,
-        0,
-    )
-
-
 def product_nn(left, right):
     left_high, left_low = split(left)
     right_high, right_low = split(right)
     both = contract(jnp.concatenate([left_high, left_low], 0), right_high, 1, 0)
     rows = left.shape[0]
     return both[:rows] + both[rows:] + contract(left_high, right_low, 1, 0)
+
+
+def product_tn(left, right):
+    return product_nn(left.T, right)
 
 
 def sandwich(gram, transfer):
@@ -182,7 +175,7 @@
         batch_ref[j, :, :count] = rows.T[:RANK, :]
         return carry
 
-    lax.fori_loop(0, RANK, step, 0, unroll=8)
+    lax.fori_loop(0, RANK, step, 0, unroll=32)
 
 
 def factor(batch_ref):
@@ -254,10 +247,12 @@
         factor_ref[pl.ds(counts[0] * RANK + j, counts[1], stride=RANK), :RANK] = values[counts[0] : sum(counts)]
         return carry
 
-    lax.fori_loop(0, RANK, step, 0, unroll=4)
+    lax.fori_loop(0, RANK, step, 0, unroll=16)
 
 
 def couple(count, blocks_ref, stage_ref, left_ref, right_ref, left_pick, right_pick, out_ref):
+    first_half = lax.broadcasted_iota(jnp.int32, (1, 128), 1) < RANK
+
     def step(group, carry):
         base = pl.multiple_of(group * 256, 256)
         stage_ref[...] = blocks_ref[pl.ds(base, 256), :].astype(F32)
@@ -268,16 +263,22 @@
             right = right_ref[right_pick(group * 8 + pair)]
             both = contract(left, square, 1, 0)
             high, low = split(both[:RANK] + both[RANK:])
-            out = contract(jnp.concatenate([high, low], 0), right[:RANK], 1, 1)
-            out = out[:RANK] + out[RANK:] + contract(high, right[RANK:], 1, 1)
-            out_ref[pl.ds(base + pair, 32, stride=8), :] = pack(out)
+            out = contract(jnp.concatenate([high, low], 0), right, 1, 0)
+            out = out[:RANK] + jnp.where(first_half, out[RANK:], 0.0)
+            out = out + pltpu.roll(out, RANK, 1)
+            out_ref[pl.ds(base + pair, 32, stride=8), :] = jnp.where(first_half, out[:32], out[32:])
         return carry
 
-    lax.fori_loop(0, count // 8, step, 0)
+    lax.fori_loop(0, count // 8, step, 0, unroll=4)
 
 
 def table_entry(value):
     return jnp.concatenate(split(value), 0)
+
+
+def right_entry(value):
+    high = value.astype(BF16).astype(F32)
+    return jnp.concatenate([high, value - high], 0).T.astype(BF16)
 
 
 STAGES = ((2, 3, 4), (4, 2, 3))
@@ -431,7 +432,7 @@
             place[pl.ds(1, 32, stride=2), :] = pltpu.roll(rows, RANK, 1)
             return carry
 
-        lax.fori_loop(0, 32, lay_out, 0, unroll=4)
+        lax.fori_loop(0, 32, lay_out, 0, unroll=16)
 
     def transfer_of(tree, m):
         return natural[tree * 32 + m][:, :RANK]
@@ -453,7 +454,7 @@
             grams[tree * LEAF_DEV + leaf, :, :RANK] = product_tn(basis, basis)
         return carry
 
-    lax.fori_loop(0, LEAF_DEV, leaf_gram, 0, unroll=4)
+    lax.fori_loop(0, LEAF_DEV, leaf_gram, 0, unroll=16)
 
     orders = (row_order, col_order)
 
@@ -467,7 +468,7 @@
             nodes[tree * 16 + q, :, :RANK] = total
         return carry
 
-    lax.fori_loop(0, 8, first_level, 0, unroll=2)
+    lax.fori_loop(0, 8, first_level, 0, unroll=8)
     source, target, offset, count = 0, 8, 16, 8
     while count > 1:
         for tree in range(2):
@@ -509,7 +510,7 @@
             copy.start()
     for leaf in range(LEAF_DEV):
         leaf_left[leaf] = table_entry(factors[leaf * RANK : (leaf + 1) * RANK, :RANK])
-        leaf_right[leaf] = table_entry(factors[(LEAF_DEV + leaf) * RANK : (LEAF_DEV + leaf + 1) * RANK, :RANK])
+        leaf_right[leaf] = right_entry(factors[(LEAF_DEV + leaf) * RANK : (LEAF_DEV + leaf + 1) * RANK, :RANK])
 
     def climb(n):
         for tree in range(2):
@@ -624,7 +625,7 @@
             grams[N_COL + line * 8 + n, :, :RANK] = unpack(col_table[line, n])
         return carry
 
-    lax.fori_loop(0, 8, spread_out, 0, unroll=2)
+    lax.fori_loop(0, 8, spread_out, 0, unroll=8)
     to_lanes(grams, batch, ROOT_BATCH)
     factor(batch)
     copies[1].wait()
@@ -639,15 +640,15 @@
     for copy in copies[4:]:
         copy.wait()
 
-    def convert(first, entries, count):
+    def convert(first, entries, count, entry):
         def step(n, carry):
-            entries[n] = table_entry(factors[pl.ds(pl.multiple_of((first + n) * RANK, RANK), RANK), :][:, :RANK])
+            entries[n] = entry(factors[pl.ds(pl.multiple_of((first + n) * RANK, RANK), RANK), :][:, :RANK])
             return carry
 
-        lax.fori_loop(0, count, step, 0, unroll=4)
-
-    convert(0, root_left, N_COL)
-    convert(N_COL, root_right, N_ROW)
+        lax.fori_loop(0, count, step, 0, unroll=16)
+
+    convert(0, root_left, N_COL, table_entry)
+    convert(N_COL, root_right, N_ROW, right_entry)
     couple(
         ROOT_PAIRS,
         root_blocks,
@@ -705,7 +706,7 @@
         vmem((RANK, RANK, 128), F32),
         vmem((2 * LEAF_DEV * RANK, 128), F32),
         vmem((LEAF_DEV, 2 * RANK, RANK), BF16),
-        vmem((LEAF_DEV, 2 * RANK, RANK), BF16),
+        vmem((LEAF_DEV, RANK, 2 * RANK), BF16),
         vmem((256, 128), F32),
         vmem((2, *packed), F32),
         vmem((2, *packed), F32),
@@ -780,7 +781,7 @@
             vmem((RANK, RANK, 128), F32),
             vmem((ROOT_BATCH * RANK, 128), F32),
             vmem((N_COL, 2 * RANK, RANK), BF16),
-            vmem((N_ROW, 2 * RANK, RANK), BF16),
+            vmem((N_ROW, RANK, 2 * RANK), BF16),
             vmem((256, 128), F32),
         ],
         compiler_params=pltpu.CompilerParams(vmem_limit_bytes=62 * 2**20),

time: 61 us -> 50.2 us (0.82)
  the two profiles are of different devices: /device:TPU:32 before, /device:TPU:16 now
where the time goes in v4:
time: 50.2 us; the launch traced here: 50 us
  Pallas kernels  49.2 us (98%)
  between operations  0.8 us (2%)
    pallas_call x1, Pallas kernels, body(): pl.pallas_call(kernel, out_shape=(shape((LEAF_PAIRS * 32, 128), F32), sha...  40.1 us
    pallas_call x1, Pallas kernels, body(): pl.pallas_call(finish, out_shape=(shape((LEAF_PAIRS * 32, 128), F32), sha...  9.12 us

profile of v4, /device:TPU:16, one launch (start us, length us, event | category | flops | bytes accessed | tf_op | source)
XLA Modules:
  0.0 50.0 jit_solution(653969327470115983)
XLA Ops:
  0.6 40.1 %shard_map.138 = (f32[2048,128]{1,0:T(8,128)}, f32[2,32,128]{2,1,0:T(8,128)}, f32[4,8,32,128]{3,2,1,0:T(8,128)}, f32[2,8,32,128]{3,2,1,0:T(8,128)}) custom-call(s32[1,1,16]{2,1,0:T(1,128)} %row_order_hbm.1, s32[1,1,16]{2,1,0:T(1,128)} %col_order_hbm.1, s32[1,2,64]{2,1,0:T(2,128)} %leaf_pattern_hbm.1, f32[512,128]{1,0:T(8,128)} %bitcast.45, ...), custom_call_target="tpu_custom_call" | custom-call | tf_op jit(solution)/shard_map/pallas_call | solution.py:733
  40.7 9.1 %shard_map.139 = (f32[2048,128]{1,0:T(8,128)}, f32[1024,128]{1,0:T(8,128)}, f32[32,128]{1,0:T(8,128)}, f32[32,128]{1,0:T(8,128)}) custom-call(f32[2048,128]{1,0:T(8,128)} %get-tuple-element.12.leaf_hbm, f32[2,32,128]{2,1,0:T(8,128)} %get-tuple-element.13.highest_hbm, f32[4,8,32,128]{3,2,1,0:T(8,128)} %get-tuple-element.14.row_table_hbm, ...), custom_call_target="tpu_custom_call" | custom-call | tf_op jit(solution)/shard_map/pallas_call | solution.py:757

commit v5 on v4

--- a/solution.py
+++ b/solution.py
@@ -80,7 +80,7 @@
     def __init__(self, depth, place, taking_part, peer, refs):
         self.depth, self.size, self.place = depth, 1 << depth, place
         self.taking_part, self.peer = taking_part, peer
-        (self.inner, self.terms, self.slots, self.inner_sent, self.inner_got, self.sent, self.got) = refs
+        (self.inner, self.paths, self.terms, self.slots, self.inner_sent, self.inner_got, self.sent, self.got) = refs
         self.level = level_of(place, depth)
         self.span = span_of(place, depth)
 
@@ -123,12 +123,16 @@
             def _(level=level):
                 self.inner_copy(0, level).wait_recv()
 
-    def make_terms(self, gram, transfer):
+    def make_paths(self, transfer):
         path = transfer
         for level in range(1, self.depth + 1):
-            self.terms[level - 1] = pack(sandwich(gram, path))
+            self.paths[level - 1] = path
             if level < self.depth:
                 path = product_nn(path, unpack(self.inner[level - 1]))
+
+    def make_terms(self, gram):
+        for level in range(1, self.depth + 1):
+            self.terms[level - 1] = pack(sandwich(gram, self.paths[level - 1]))
 
     def term_copy(self, target, sender):
         return pltpu.make_async_remote_copy(
@@ -418,8 +422,8 @@
     for tree in range(2):
         stages.append([])
         for n in range(3):
-            at = 7 * (3 * tree + n)
-            stages[tree].append(Stage(STAGES[tree][n], *layout[tree][n], stage_refs[at : at + 7]))
+            at = 8 * (3 * tree + n)
+            stages[tree].append(Stage(STAGES[tree][n], *layout[tree][n], stage_refs[at : at + 8]))
 
     for copy in copies[:2]:
         copy.wait()
@@ -469,6 +473,10 @@
         return carry
 
     lax.fori_loop(0, 8, first_level, 0, unroll=8)
+    for tree in range(2):
+        stages[tree][0].receive_inner()
+    for tree in range(2):
+        stages[tree][0].make_paths(transfer_of(tree, 30))
     source, target, offset, count = 0, 8, 16, 8
     while count > 1:
         for tree in range(2):
@@ -489,8 +497,7 @@
 
     for tree in range(2):
         stage = stages[tree][0]
-        stage.receive_inner()
-        stage.make_terms(roots[tree], transfer_of(tree, 30))
+        stage.make_terms(roots[tree])
         stage.send_terms()
 
     for tree in range(2):
@@ -503,6 +510,15 @@
     to_lanes(grams, batch, 2 * LEAF_DEV)
     factor(batch)
     from_lanes(batch, factors, (LEAF_DEV, LEAF_DEV))
+    for n in range(1, 3):
+        for tree in range(2):
+            stage, before = stages[tree][n], stages[tree][n - 1]
+            stage.receive_inner()
+
+            @pl.when(stage.taking_part)
+            def _(stage=stage, before=before):
+                stage.make_paths(unpack(before.inner[before.depth - 1]))
+
     for tree in range(2):
         for k in range(1, 8):
             line_copy(tree, k, lax.rem(line_places[tree] + 8 - k, 8)).wait_recv()
@@ -516,12 +532,10 @@
         for tree in range(2):
             stages[tree][n - 1].receive_terms(highest.at[tree])
             stage = stages[tree][n]
-            stage.receive_inner()
 
             @pl.when(stage.taking_part)
-            def _(stage=stage, tree=tree, n=n):
-                exit_transfer = unpack(stages[tree][n - 1].inner[stages[tree][n - 1].depth - 1])
-                stage.make_terms(unpack(highest[tree]), exit_transfer)
+            def _(stage=stage, tree=tree):
+                stage.make_terms(unpack(highest[tree]))
 
             stage.send_terms()
 
@@ -723,6 +737,7 @@
             size = 1 << depth
             scratch += [
                 vmem((depth, *packed), F32),
+                vmem((depth, RANK, RANK), F32),
                 vmem((depth, *packed), F32),
                 vmem((size, *packed), F32),
                 dma((size,)),

time: 50.2 us -> 50.7 us (level)
  no operation moved by 1% of the time
where the time goes in v5:
time: 50.7 us; the launch traced here: 50.5 us
  Pallas kernels  49.7 us (98%)
  between operations  0.8 us (2%)
    pallas_call x1, Pallas kernels, body(): pl.pallas_call(kernel, out_shape=(shape((LEAF_PAIRS * 32, 128), F32), sha...  40.6 us
    pallas_call x1, Pallas kernels, body(): pl.pallas_call(finish, out_shape=(shape((LEAF_PAIRS * 32, 128), F32), sha...  9.12 us

profile of v5, /device:TPU:16, one launch (start us, length us, event | category | flops | bytes accessed | tf_op | source)
XLA Modules:
  0.0 50.5 jit_solution(12077176150074091449)
XLA Ops:
  0.6 40.6 %shard_map.138 = (f32[2048,128]{1,0:T(8,128)}, f32[2,32,128]{2,1,0:T(8,128)}, f32[4,8,32,128]{3,2,1,0:T(8,128)}, f32[2,8,32,128]{3,2,1,0:T(8,128)}) custom-call(s32[1,1,16]{2,1,0:T(1,128)} %row_order_hbm.1, s32[1,1,16]{2,1,0:T(1,128)} %col_order_hbm.1, s32[1,2,64]{2,1,0:T(2,128)} %leaf_pattern_hbm.1, f32[512,128]{1,0:T(8,128)} %bitcast.45, ...), custom_call_target="tpu_custom_call" | custom-call | tf_op jit(solution)/shard_map/pallas_call | solution.py:748
  41.2 9.1 %shard_map.139 = (f32[2048,128]{1,0:T(8,128)}, f32[1024,128]{1,0:T(8,128)}, f32[32,128]{1,0:T(8,128)}, f32[32,128]{1,0:T(8,128)}) custom-call(f32[2048,128]{1,0:T(8,128)} %get-tuple-element.12.leaf_hbm, f32[2,32,128]{2,1,0:T(8,128)} %get-tuple-element.13.highest_hbm, f32[4,8,32,128]{3,2,1,0:T(8,128)} %get-tuple-element.14.row_table_hbm, ...), custom_call_target="tpu_custom_call" | custom-call | tf_op jit(solution)/shard_map/pallas_call | solution.py:772
